TPU v7x, 32 devices: a whole 2x2x4 slice. The times are simulated.
32 devices in a mesh: row: 4 (over z), col: 4 (over y, core), mode: 2 (over x).
Axes of the slice: x: 2, y: 2, z: 4, core: 2. Of those that a mesh axis runs over, the one named last changes fastest.
Arguments:
- objects: float32 [2, 2, 1024, 1024], P(None, None, 'row', 'col'), may hold values from -4 to 4
- probes: float32 [2, 2, 128, 128], P('mode'), may hold values from -3 to 3
- phase: float32 [128, 128], replicated, may hold values from -3.140625 to 3.140625
- offsets: int32 [4, 4, 8, 2], P('row', 'col'), may hold values from 0 to 255
- measured: float32 [4, 4, 8, 128, 128], P('row', 'col'), may hold values from 0 to 2
Outputs:
- gradient: float32 [2, 2, 1024, 1024], P(None, None, 'row', 'col')
Inputs may be any that keep to these rules, and one draw needn't show every extreme that they name: `offsets`: windows start inside their own tile of 256 x 256 cells and reach up to 127 cells into the next tiles down and to the right.
All inputs are finite; a program needn't handle non-finite values.
Results may differ from a plain program's by a relative error of at most 0.0001.
Values sent between devices are 32-bit elements; how exact they have to be, the bound alone decides.
No kernel may reach another device: no remote copies, remote signals or barrier semaphores. Data moves between devices by JAX's collectives and lax.ppermute only.
A program may use at most 64 MiB of HBM per device.

v0:
```python
import functools
import math

import jax
import jax.numpy as jnp
import numpy as np
from jax import lax
from jax.experimental import pallas as pl
from jax.experimental.pallas import tpu as pltpu
from jax.sharding import PartitionSpec as P

F32 = jnp.float32
BF16 = jnp.bfloat16
FORWARD, INVERSE = 0, 1
GROUP = 4
VMEM = pl.BlockSpec(memory_space=pltpu.VMEM)
SMEM = pl.BlockSpec(memory_space=pltpu.SMEM)


def passed_along(value, axis, by):
    count = lax.axis_size(axis)
    pairs = [(i, i + by) for i in range(count) if 0 <= i + by < count]
    return lax.ppermute(value, axis, pairs)


def passed_across(value, by):
    rows, cols = lax.axis_size("row"), lax.axis_size("col")
    pairs = [
        (r * cols + c, (r + by) * cols + c + by)
        for r in range(rows)
        for c in range(cols)
        if 0 <= r + by < rows and 0 <= c + by < cols
    ]
    return lax.ppermute(value, ("row", "col"), pairs)


def tables(length):
    counter = np.arange(length)
    angle = (counter[:, None] * counter[None, :] % length) * (2.0 * math.pi / length)
    cos, sin = np.cos(angle) / math.sqrt(length), np.sin(angle) / math.sqrt(length)
    forward = np.block([[cos, -sin], [sin, cos]])
    kept = []
    for table in (forward, forward.T):
        high = table.astype(jnp.bfloat16)
        kept.append(np.stack([high, (table - high.astype(np.float64)).astype(jnp.bfloat16)]))
    return jnp.asarray(np.stack(kept))


def parts(value):
    high = value.astype(BF16)
    return high, (value - high.astype(F32)).astype(BF16)


def fourier(modes, way, table):
    n = modes[0][0].shape[0]
    right_high, right_low = table[way, 0], table[way, 1]
    left_high, left_low = table[1 - way, 0], table[1 - way, 1]
    high, low = parts(jnp.concatenate([jnp.concatenate(pair, 1) for pair in modes], 0))
    rows = jnp.dot(
        jnp.concatenate([high, low, high], 1),
        jnp.concatenate([right_high, right_high, right_low], 0),
        preferred_element_type=F32,
    )
    stacked = [
        jnp.concatenate([rows[i * n : (i + 1) * n, :n], rows[i * n : (i + 1) * n, n:]], 0) for i in range(len(modes))
    ]
    high, low = parts(jnp.concatenate(stacked, 1))
    both = jnp.dot(
        jnp.concatenate([left_high, left_high, left_low], 1),
        jnp.concatenate([high, low, high], 0),
        preferred_element_type=F32,
    )
    return [(both[:n, i * n : (i + 1) * n], both[n:, i * n : (i + 1) * n]) for i in range(len(modes))]


def times(a, b):
    return a[0] * b[0] - a[1] * b[1], a[0] * b[1] + a[1] * b[0]


def times_conj(a, b):
    return a[0] * b[0] + a[1] * b[1], a[1] * b[0] - a[0] * b[1]


def summed(values):
    return functools.reduce(lambda a, b: a + b, values)


def place_of(offsets, position, n):
    row, col = offsets[position, 0], offsets[position, 1]
    rows = pl.ds(pl.multiple_of(row // 8 * 8, 8), n + 8)
    cols = pl.ds(pl.multiple_of(col // n * n, n), 2 * n)
    return rows, cols, row % 8, col % n


def cut(source, channel, place, n):
    rows, cols, down, across = place
    groups = n // 8
    lane = lax.broadcasted_iota(jnp.int32, (groups + 1, 8, n), 2)
    line = lax.broadcasted_iota(jnp.int32, (groups, 8, n), 1)
    wide = source[channel, rows, cols]
    turn = (n - across) % n
    first = pltpu.roll(wide[:, :n].reshape(groups + 1, 8, n), turn, 2)
    second = pltpu.roll(wide[:, n:].reshape(groups + 1, 8, n), turn, 2)
    tall = pltpu.roll(jnp.where(lane < n - across, first, second), (8 - down) % 8, 1)
    return jnp.where(line < 8 - down, tall[:groups], tall[1:]).reshape(n, n)


def deposit(target, channel, place, value):
    rows, cols, down, across = place
    n = value.shape[0]
    groups = n // 8
    lane = lax.broadcasted_iota(jnp.int32, (groups + 1, 8, n), 2)
    line = lax.broadcasted_iota(jnp.int32, (groups + 1, 8, n), 1)
    turned = pltpu.roll(value.reshape(groups, 8, n), down, 1)
    blank = jnp.zeros((1, 8, n), F32)
    tall = jnp.where(line >= down, jnp.concatenate([turned, blank], 0), jnp.concatenate([blank, turned], 0))
    tall = pltpu.roll(tall, across, 2)
    zero = jnp.zeros_like(tall)
    first = jnp.where(lane >= across, tall, zero).reshape(n + 8, n)
    second = jnp.where(lane < across, tall, zero).reshape(n + 8, n)
    target[channel, rows, cols] += jnp.concatenate([first, second], 1)


def cut_pair(source, place, n):
    return cut(source, 0, place, n), cut(source, 1, place, n)


def deposit_pair(target, place, terms):
    for channel in range(2):
        deposit(target, channel, place, summed([term[channel] for term in terms]))


def keep(target, position, modes):
    for m, (re, im) in enumerate(modes):
        target[position, m, 0] = re
        target[position, m, 1] = im


def kept(source, position):
    return [(source[position, m, 0], source[position, m, 1]) for m in range(source.shape[1])]


def groups_of(count):
    return [range(k, min(k + GROUP, count)) for k in range(0, count, GROUP)]


def join(extended, tile, right, lower, corner):
    t = tile.shape[-1]
    extended[:, :t, :t] = tile[...]
    extended[:, :t, t:] = right[...]
    extended[:, t:, :t] = lower[...]
    extended[:, t:, t:] = corner[...]


def part_ways(total, own, right, lower, corner):
    t = own.shape[-1]
    own[...] = total[:, :t, :t]
    right[...] = total[:, :t, t:]
    lower[...] = total[:, t:, :t]
    corner[...] = total[:, t:, t:]


def pack_kernel(objects, tile, lower0, corner, right0):
    n = corner.shape[-1]
    lower0[...] = objects[0, :, :n, :]
    corner[...] = objects[:, :, :n, :n]
    right0[...] = objects[0, :, :, :n]
    tile[...] = objects[...]


def stage_kernel(tile, table, lower1, right1, table_out):
    n = right1.shape[-1]
    lower1[...] = tile[1, :, :n, :]
    right1[...] = tile[1, :, :, :n]
    table_out[...] = table[...]


def factor_kernel(*refs):
    phase, out = refs[-2:]
    for m, probe in enumerate(refs[:-2]):
        out[m] = probe[...]
    out[len(refs) - 2, 0] = jnp.cos(phase[...])
    out[len(refs) - 2, 1] = jnp.sin(phase[...])


def factors_of(factors):
    pairs = [(factors[m, 0], factors[m, 1]) for m in range(factors.shape[0])]
    return pairs[:-1], pairs[-1]


def middle_kernel(offsets, objects, right, lower, corner, factors, table, middle, extended):
    n = corner.shape[-1]
    join(extended, objects.at[0], right, lower, corner.at[0])
    probes, spread = factors_of(factors)
    for group in groups_of(offsets.shape[0]):
        windows = [cut_pair(extended, place_of(offsets, k, n), n) for k in group]
        waves = [[times(p, window) for p in probes] for window in windows]
        waves = [fourier(wave, FORWARD, table) for wave in waves]
        waves = [[times(w, spread) for w in wave] for wave in waves]
        waves = [fourier(wave, INVERSE, table) for wave in waves]
        for k, wave in zip(group, waves):
            keep(middle, k, wave)


def second_kernel(
    offsets, objects, right, lower, corner, middle, measured, table,
    back, own, rim_right, rim_lower, rim_corner, extended, total,
):
    n = corner.shape[-1]
    join(extended, objects.at[1], right, lower, corner.at[1])
    total[...] = jnp.zeros_like(total)
    for group in groups_of(offsets.shape[0]):
        windows = [cut_pair(extended, place_of(offsets, k, n), n) for k in group]
        waves = [kept(middle, k) for k in group]
        far = [[times(w, window) for w in wave] for wave, window in zip(waves, windows)]
        far = [fourier(wave, FORWARD, table) for wave in far]
        grads = []
        for k, wave in zip(group, far):
            resid = 4.0 * (summed([re * re + im * im for re, im in wave]) - measured[k])
            grads.append([(resid * re, resid * im) for re, im in wave])
        grads = [fourier(grad, INVERSE, table) for grad in grads]
        for k, grad, window in zip(group, grads, windows):
            keep(back, k, [times_conj(g, window) for g in grad])
        for k, grad, wave in zip(group, grads, waves):
            deposit_pair(total, place_of(offsets, k, n), [times_conj(g, w) for g, w in zip(grad, wave)])
    part_ways(total, own, rim_right, rim_lower, rim_corner)


def first_kernel(
    offsets, back, factors, table, other_right, other_corner, own, rim_right, rim_lower, rim_corner, total
):
    n = rim_corner.shape[-1]
    probes, spread = factors_of(factors)
    total[...] = jnp.zeros_like(total)
    rim_right[1] = other_right[...]
    rim_corner[1] = other_corner[...]
    for group in groups_of(offsets.shape[0]):
        waves = [fourier(kept(back, k), FORWARD, table) for k in group]
        waves = [[times_conj(w, spread) for w in wave] for wave in waves]
        waves = [fourier(wave, INVERSE, table) for wave in waves]
        for k, wave in zip(group, waves):
            deposit_pair(total, place_of(offsets, k, n), [times_conj(w, p) for w, p in zip(wave, probes)])
    part_ways(total, own, rim_right.at[0], rim_lower, rim_corner.at[0])


def add_lower_kernel(own, lower, out):
    n = lower.shape[-2]
    out[:, n:] = own[:, n:]
    out[:, :n] = own[:, :n] + lower[...]


def combine_kernel(own0, own1, right, lower0, corner, out):
    n = corner.shape[-1]
    out[0] = own0[...]
    out[1] = own1[...]
    out[0, :, :n, :] += lower0[...]
    for s in range(out.shape[0]):
        out[s, :, :, :n] += right[s]
        out[s, :, :n, :n] += corner[s]


def cost(transforms, n):
    return pl.CostEstimate(flops=transforms * 24 * n * n * n, bytes_accessed=1 << 22, transcendentals=0)


def on_device(objects, probes, phase, offsets, measured):
    slices, _, t, _ = objects.shape
    n = probes.shape[2]
    reach = t + n
    mode_count = lax.axis_size("mode")
    starts, targets = offsets[0, 0], measured[0, 0]
    count = starts.shape[0]
    shape = lambda *dims: jax.ShapeDtypeStruct(dims, F32)
    params = pltpu.CompilerParams(vmem_limit_bytes=40 << 20)
    rim_right, rim_lower, rim_corner = shape(slices, 2, t, n), shape(2, n, t), shape(slices, 2, n, n)

    tile, lower0, corner, right0 = pl.pallas_call(
        pack_kernel,
        out_shape=(shape(*objects.shape), rim_lower, rim_corner, shape(2, t, n)),
        in_specs=[VMEM],
        out_specs=(VMEM,) * 4,
        compiler_params=params,
    )(objects)
    lower0 = passed_along(lower0, "row", -1)
    corner = passed_across(corner, -1)
    right0 = passed_along(right0, "col", -1)
    received = []
    for by in range(1, mode_count):
        received.append(lax.ppermute(probes, "mode", [(i, (i + by) % mode_count) for i in range(mode_count)])[0])

    table = tables(n)
    lower1, right1, table = pl.pallas_call(
        stage_kernel,
        out_shape=(rim_lower, shape(2, t, n), jax.ShapeDtypeStruct(table.shape, table.dtype)),
        in_specs=[VMEM] * 2,
        out_specs=(VMEM,) * 3,
        compiler_params=params,
    )(tile, table)
    lower1 = passed_along(lower1, "row", -1)
    right1 = passed_along(right1, "col", -1)
    factors = pl.pallas_call(
        factor_kernel,
        out_shape=shape(mode_count + 1, 2, n, n),
        in_specs=[VMEM] * (mode_count + 1),
        out_specs=VMEM,
        compiler_params=params,
    )(probes[0], *received, phase)
    waves = shape(count, mode_count, 2, n, n)
    window_area = pltpu.VMEM((2, reach, reach), F32)
    middle = pl.pallas_call(
        middle_kernel,
        out_shape=waves,
        in_specs=[SMEM] + [VMEM] * 6,
        out_specs=VMEM,
        scratch_shapes=[window_area],
        compiler_params=params,
        cost_estimate=cost(12 * count * mode_count, n),
    )(starts, tile, right0, lower0, corner, factors, table)

    back, own1, grad_right, grad_lower1, grad_corner = pl.pallas_call(
        second_kernel,
        out_shape=(waves, shape(2, t, t), shape(2, t, n), rim_lower, shape(2, n, n)),
        in_specs=[SMEM] + [VMEM] * 7,
        out_specs=(VMEM,) * 5,
        scratch_shapes=[window_area] * 2,
        compiler_params=params,
        cost_estimate=cost(6 * count * mode_count, n),
    )(starts, tile, right1, lower1, corner, middle, targets, table)
    grad_lower1 = passed_along(grad_lower1, "row", 1)

    own0, grad_right, grad_lower0, grad_corner = pl.pallas_call(
        first_kernel,
        out_shape=(shape(2, t, t), rim_right, rim_lower, rim_corner),
        in_specs=[SMEM] + [VMEM] * 5,
        out_specs=(VMEM,) * 4,
        scratch_shapes=[window_area],
        compiler_params=params,
        cost_estimate=cost(6 * count * mode_count, n),
    )(starts, back, factors, table, grad_right, grad_corner)
    grad_lower0 = passed_along(grad_lower0, "row", 1)
    grad_right = passed_along(grad_right, "col", 1)
    grad_corner = passed_across(grad_corner, 1)

    own1 = pl.pallas_call(
        add_lower_kernel,
        out_shape=shape(2, t, t),
        in_specs=[VMEM] * 2,
        out_specs=VMEM,
        input_output_aliases={0: 0},
        compiler_params=params,
        cost_estimate=cost(64, n),
    )(own1, grad_lower1)
    return pl.pallas_call(
        combine_kernel,
        out_shape=jax.ShapeDtypeStruct(objects.shape, F32),
        in_specs=[VMEM] * 5,
        out_specs=VMEM,
        compiler_params=params,
    )(own0, own1, grad_right, grad_lower0, grad_corner)


def solution(mesh):
    placed = (
        P(None, None, "row", "col"),
        P("mode", None, None, None),
        P(),
        P("row", "col", None, None),
        P("row", "col", None, None, None),
    )
    return jax.shard_map(
        on_device,
        mesh=mesh,
        in_specs=placed,
        out_specs=P(None, None, "row", "col"),
        check_vma=False,
    )
```

profile of v0, /device:TPU:0, one launch (start us, length us, event | category | flops | bytes accessed | tf_op | source)
XLA Modules:
  0.0 56.7 jit_solution(11205532945925452067)
XLA Ops:
  0.0 0.0 copy-start
  0.0 1.2 %copy-done = f32[2,2,256,256]{3,2,1,0:T(8,128)S(1)} copy-done((f32[2,2,256,256]{3,2,1,0:T(8,128)S(1)}, f32[2,2,256,256]{3,2,1,0:T(8,128)}, u32[]{:S(2)}) %copy-start) | copy-done | bytes 1048600
  1.2 0.0 copy-start.6
  1.2 0.0 copy-start.2
  1.2 0.0 copy-start.3
  1.2 0.1 shard_map.64
  1.4 1.3 %collective-permute-start.2 = (f32[2,2,128,128]{3,2,1,0:T(8,128)S(1)}, f32[2,2,128,128]{3,2,1,0:T(8,128)S(1)}, u32[]{:S(2)}, u32[]{:S(2)}) collective-permute-start(f32[2,2,128,128]{3,2,1,0:T(8,128)S(1)} %get-tuple-element.24), channel_id=1, source_target_pairs={{10,0},{12,2},{14,4},{18,8},{20,10},{22,12},{26,16},{28,18},{30,20... | collective-permute-start | bytes 786440 | tf_op jit(solution)/shard_map/ppermute | solution.py:34
  2.7 1.3 %collective-permute-start.3 = (f32[2,256,128]{2,1,0:T(8,128)S(1)}, f32[2,256,128]{2,1,0:T(8,128)S(1)}, u32[]{:S(2)}, u32[]{:S(2)}) collective-permute-start(f32[2,256,128]{2,1,0:T(8,128)S(1)} %get-tuple-element.25), channel_id=1, source_target_pairs={{2,0},{4,2},{6,4},{3,1},{5,3},{7,5},{10,8},{12,10},{14,12},{11,9},... | collective-permute-start | bytes 786440 | tf_op jit(solution)/shard_map/ppermute | solution.py:23
  4.0 1.3 %collective-permute-start.4 = (f32[2,128,256]{2,1,0:T(8,128)S(1)}, f32[2,128,256]{2,1,0:T(8,128)}, u32[]{:S(2)}, u32[]{:S(2)}) collective-permute-start(f32[2,128,256]{2,1,0:T(8,128)S(1)} %get-tuple-element.26), channel_id=1, source_target_pairs={{8,0},{16,8},{24,16},{9,1},{17,9},{25,17},{10,2},{18,10},{26,18},{... | collective-permute-start | bytes 786440 | tf_op jit(solution)/shard_map/ppermute | solution.py:23
  5.3 3.0 %collective-permute-start.5 = (f32[1,2,128,128]{3,2,1,0:T(8,128)}, f32[1,2,128,128]{3,2,1,0:T(8,128)S(1)}, u32[]{:S(2)}, u32[]{:S(2)}) collective-permute-start(f32[1,2,128,128]{3,2,1,0:T(8,128)} %param.7), channel_id=1, source_target_pairs={{0,1},{1,0},{2,3},{3,2},{4,5},{5,4},{6,7},{7,6},{8,9},{9,8},{10,11... | collective-permute-start | bytes 393224 | tf_op jit(solution)/shard_map/ppermute | solution.py:289
  8.3 0.0 copy-start.1
  8.3 1.0 %copy-done.1 = bf16[2,2,256,256]{3,2,1,0:T(8,128)(2,1)S(1)} copy-done((bf16[2,2,256,256]{3,2,1,0:T(8,128)(2,1)S(1)}, bf16[2,2,256,256]{3,2,1,0:T(8,128)(2,1)}, u32[]{:S(2)}) %copy-start.1) | copy-done | bytes 524312
  9.3 0.8 %shard_map.65 = (f32[2,128,256]{2,1,0:T(8,128)S(1)}, f32[2,256,128]{2,1,0:T(8,128)}, bf16[2,2,256,256]{3,2,1,0:T(8,128)(2,1)S(1)}) custom-call(f32[2,2,256,256]{3,2,1,0:T(8,128)S(1)} %get-tuple-element.21.tile.objects, bf16[2,2,256,256]{3,2,1,0:T(8,128)(2,1)S(1)} %copy-done.1), custom_call_target="tpu_custom_call" | custom-call | tf_op jit(solution)/shard_map/pallas_call | solution.py:292
  10.1 0.0 copy-start.5
  10.1 0.7 %copy-done.5 = f32[2,128,256]{2,1,0:T(8,128)} copy-done((f32[2,128,256]{2,1,0:T(8,128)}, f32[2,128,256]{2,1,0:T(8,128)S(1)}, u32[]{:S(2)}) %copy-start.5) | copy-done | bytes 262168
  10.8 1.3 %collective-permute-start = (f32[2,256,128]{2,1,0:T(8,128)}, f32[2,256,128]{2,1,0:T(8,128)S(1)}, u32[]{:S(2)}, u32[]{:S(2)}) collective-permute-start(f32[2,256,128]{2,1,0:T(8,128)} %get-tuple-element.22), channel_id=1, source_target_pairs={{2,0},{4,2},{6,4},{3,1},{5,3},{7,5},{10,8},{12,10},{14,12},{11,9},... | collective-permute-start | bytes 786440 | tf_op jit(solution)/shard_map/ppermute | solution.py:23
  12.1 0.0 copy-done.6
  12.1 0.1 copy.10.offsets
  12.2 0.3 collective-permute-done.5
  12.5 1.3 %collective-permute-start.1 = (f32[2,128,256]{2,1,0:T(8,128)}, f32[2,128,256]{2,1,0:T(8,128)S(1)}, u32[]{:S(2)}, u32[]{:S(2)}) collective-permute-start(f32[2,128,256]{2,1,0:T(8,128)} %copy-done.5), channel_id=1, source_target_pairs={{8,0},{16,8},{24,16},{9,1},{17,9},{25,17},{10,2},{18,10},{26,18},{... | collective-permute-start | bytes 786440 | tf_op jit(solution)/shard_map/ppermute | solution.py:23
  13.8 0.0 copy-done.2
  13.8 0.0 copy-done.3
  13.8 0.4 shard_map.66.factors
  14.2 0.0 collective-permute-done.2.corner
  14.2 0.0 collective-permute-done.3.right
  14.2 1.5 %collective-permute-done.4.lower = f32[2,128,256]{2,1,0:T(8,128)} collective-permute-done((f32[2,128,256]{2,1,0:T(8,128)S(1)}, f32[2,128,256]{2,1,0:T(8,128)}, u32[]{:S(2)}, u32[]{:S(2)}) %collective-permute-start.4) | collective-permute-done | bytes 262176 | tf_op jit(solution)/shard_map/ppermute | solution.py:23
  15.8 0.0 copy-start.4
  15.8 5.0 %shard_map.67.middle = f32[8,2,2,128,128]{4,3,2,1,0:T(8,128)S(1)} custom-call(s32[8,2]{1,0:T(8,128)S(1)} %copy.10.offsets, f32[2,2,256,256]{3,2,1,0:T(8,128)S(1)} %get-tuple-element.21.tile.objects, f32[2,256,128]{2,1,0:T(8,128)S(1)} %collective-permute-done.3.right, f32[2,128,256]{2,1,0:T(8,128)} %collective-permute-done.4.lower, ...), custom_call_target="tpu_custom_call" | custom-call | flops 9663676416 | bytes 4194304 | tf_op jit(solution)/shard_map/pallas_call | solution.py:310
  20.8 0.0 collective-permute-done.right
  20.9 2.6 %collective-permute-done.1.lower = f32[2,128,256]{2,1,0:T(8,128)S(1)} collective-permute-done((f32[2,128,256]{2,1,0:T(8,128)}, f32[2,128,256]{2,1,0:T(8,128)S(1)}, u32[]{:S(2)}, u32[]{:S(2)}) %collective-permute-start.1) | collective-permute-done | bytes 262176 | tf_op jit(solution)/shard_map/ppermute | solution.py:23
  23.5 0.0 copy-done.4
  23.5 5.2 %shard_map.68 = (f32[8,2,2,128,128]{4,3,2,1,0:T(8,128)S(1)}, f32[2,256,256]{2,1,0:T(8,128)S(1)}, f32[2,256,128]{2,1,0:T(8,128)S(1)}, f32[2,128,256]{2,1,0:T(8,128)S(1)}, f32[2,128,128]{2,1,0:T(8,128)S(1)}) custom-call(s32[8,2]{1,0:T(8,128)S(1)} %copy.10.offsets, f32[2,2,256,256]{3,2,1,0:T(8,128)S(1)} %get-tuple-element.21.tile.objects, ...), custom_call_target="tpu_custom_call" | custom-call | flops 4831838208 | bytes 4194304 | tf_op jit(solution)/shard_map/pallas_call | solution.py:320
  28.7 4.8 %collective-permute-start.6 = (f32[2,128,256]{2,1,0:T(8,128)S(1)}, f32[2,128,256]{2,1,0:T(8,128)S(1)}, u32[]{:S(2)}, u32[]{:S(2)}) collective-permute-start(f32[2,128,256]{2,1,0:T(8,128)S(1)} %get-tuple-element.33), channel_id=1, source_target_pairs={{0,8},{8,16},{16,24},{1,9},{9,17},{17,25},{2,10},{10,18},{18,26},{... | collective-permute-start | bytes 786440 | tf_op jit(solution)/shard_map/ppermute | solution.py:23
  33.5 4.9 %shard_map.69 = (f32[2,256,256]{2,1,0:T(8,128)S(1)}, f32[2,2,256,128]{3,2,1,0:T(8,128)S(1)}, f32[2,128,256]{2,1,0:T(8,128)S(1)}, f32[2,2,128,128]{3,2,1,0:T(8,128)S(1)}) custom-call(s32[8,2]{1,0:T(8,128)S(1)} %copy.10.offsets, f32[8,2,2,128,128]{4,3,2,1,0:T(8,128)S(1)} %get-tuple-element.28.back, f32[3,2,128,128]{3,2,1,0:T(8,128)S(1)} %shard_map.66.factors, ...), custom_call_target="tpu_custom_call" | custom-call | flops 4831838208 | bytes 4194304 | tf_op jit(solution)/shard_map/pallas_call | solution.py:331
  38.3 1.8 %collective-permute-start.7 = (f32[2,2,256,128]{3,2,1,0:T(8,128)S(1)}, f32[2,2,256,128]{3,2,1,0:T(8,128)S(1)}, u32[]{:S(2)}, u32[]{:S(2)}) collective-permute-start(f32[2,2,256,128]{3,2,1,0:T(8,128)S(1)} %get-tuple-element.34), channel_id=1, source_target_pairs={{0,2},{2,4},{4,6},{1,3},{3,5},{5,7},{8,10},{10,12},{12,14},{9,11},... | collective-permute-start | bytes 1572872 | tf_op jit(solution)/shard_map/ppermute | solution.py:23
  40.1 4.2 %collective-permute-start.8 = (f32[2,128,256]{2,1,0:T(8,128)S(1)}, f32[2,128,256]{2,1,0:T(8,128)S(1)}, u32[]{:S(2)}, u32[]{:S(2)}) collective-permute-start(f32[2,128,256]{2,1,0:T(8,128)S(1)} %get-tuple-element.35), channel_id=1, source_target_pairs={{0,8},{8,16},{16,24},{1,9},{9,17},{17,25},{2,10},{10,18},{18,26},{... | collective-permute-start | bytes 786440 | tf_op jit(solution)/shard_map/ppermute | solution.py:23
  44.3 4.5 %collective-permute-start.9 = (f32[2,2,128,128]{3,2,1,0:T(8,128)S(1)}, f32[2,2,128,128]{3,2,1,0:T(8,128)S(1)}, u32[]{:S(2)}, u32[]{:S(2)}) collective-permute-start(f32[2,2,128,128]{3,2,1,0:T(8,128)S(1)} %get-tuple-element.36), channel_id=1, source_target_pairs={{0,10},{2,12},{4,14},{8,18},{10,20},{12,22},{16,26},{18,28},{20,30... | collective-permute-start | bytes 786440 | tf_op jit(solution)/shard_map/ppermute | solution.py:34
  48.9 0.0 collective-permute-done.6.lower
  48.9 0.1 shard_map.70.own1
  49.0 0.0 collective-permute-done.8.lower0
  49.0 6.6 %collective-permute-done.9.corner = f32[2,2,128,128]{3,2,1,0:T(8,128)S(1)} collective-permute-done((f32[2,2,128,128]{3,2,1,0:T(8,128)S(1)}, f32[2,2,128,128]{3,2,1,0:T(8,128)S(1)}, u32[]{:S(2)}, u32[]{:S(2)}) %collective-permute-start.9) | collective-permute-done | bytes 262176 | tf_op jit(solution)/shard_map/ppermute | solution.py:34
  55.6 0.0 collective-permute-done.7.right
  55.6 1.1 %shard_map.71 = f32[2,2,256,256]{3,2,1,0:T(8,128)} custom-call(f32[2,256,256]{2,1,0:T(8,128)S(1)} %get-tuple-element.31.own0, f32[2,256,256]{2,1,0:T(8,128)S(1)} %shard_map.70.own1, f32[2,2,256,128]{3,2,1,0:T(8,128)S(1)} %collective-permute-done.7.right, f32[2,128,256]{2,1,0:T(8,128)S(1)} %collective-permute-done.8.lower0, ...), custom_call_target="tpu_custom_call" | custom-call | tf_op jit(solution)/shard_map/pallas_call | solution.py:353
Async XLA Ops:
  0.0 1.2 %copy-start = (f32[2,2,256,256]{3,2,1,0:T(8,128)S(1)}, f32[2,2,256,256]{3,2,1,0:T(8,128)}, u32[]{:S(2)}) copy-start(f32[2,2,256,256]{3,2,1,0:T(8,128)} %objects.1) | copy-start | bytes 3145732
  1.2 10.8 %copy-start.6 = (s32[1,1,8,2]{2,3,1,0:T(2,128)S(1)}, s32[1,1,8,2]{2,3,1,0:T(2,128)}, u32[]{:S(2)}) copy-start(s32[1,1,8,2]{2,3,1,0:T(2,128)} %param.9) | copy-start | bytes 196
  1.2 12.5 %copy-start.2 = (f32[1,2,128,128]{3,2,1,0:T(8,128)S(1)}, f32[1,2,128,128]{3,2,1,0:T(8,128)}, u32[]{:S(2)}) copy-start(f32[1,2,128,128]{3,2,1,0:T(8,128)} %param.7) | copy-start | bytes 393220
  1.2 12.5 %copy-start.3 = (f32[128,128]{1,0:T(8,128)S(1)}, f32[128,128]{1,0:T(8,128)}, u32[]{:S(2)}) copy-start(f32[128,128]{1,0:T(8,128)} %refs_2_.1) | copy-start | bytes 196612
  1.4 12.9 %collective-permute-start.2 = (f32[2,2,128,128]{3,2,1,0:T(8,128)S(1)}, f32[2,2,128,128]{3,2,1,0:T(8,128)S(1)}, u32[]{:S(2)}, u32[]{:S(2)}) collective-permute-start(f32[2,2,128,128]{3,2,1,0:T(8,128)S(1)} %get-tuple-element.24), channel_id=1, source_target_pairs={{10,0},{12,2},{14,4},{18,8},{20,10},{22,12},{26,16},{28,18},{30,20... | collective-permute-start | bytes 786440 | tf_op jit(solution)/shard_map/ppermute | solution.py:34
  2.7 11.6 %collective-permute-start.3 = (f32[2,256,128]{2,1,0:T(8,128)S(1)}, f32[2,256,128]{2,1,0:T(8,128)S(1)}, u32[]{:S(2)}, u32[]{:S(2)}) collective-permute-start(f32[2,256,128]{2,1,0:T(8,128)S(1)} %get-tuple-element.25), channel_id=1, source_target_pairs={{2,0},{4,2},{6,4},{3,1},{5,3},{7,5},{10,8},{12,10},{14,12},{11,9},... | collective-permute-start | bytes 786440 | tf_op jit(solution)/shard_map/ppermute | solution.py:23
  4.0 11.8 %collective-permute-start.4 = (f32[2,128,256]{2,1,0:T(8,128)S(1)}, f32[2,128,256]{2,1,0:T(8,128)}, u32[]{:S(2)}, u32[]{:S(2)}) collective-permute-start(f32[2,128,256]{2,1,0:T(8,128)S(1)} %get-tuple-element.26), channel_id=1, source_target_pairs={{8,0},{16,8},{24,16},{9,1},{17,9},{25,17},{10,2},{18,10},{26,18},{... | collective-permute-start | bytes 786440 | tf_op jit(solution)/shard_map/ppermute | solution.py:23
  5.3 7.2 %collective-permute-start.5 = (f32[1,2,128,128]{3,2,1,0:T(8,128)}, f32[1,2,128,128]{3,2,1,0:T(8,128)S(1)}, u32[]{:S(2)}, u32[]{:S(2)}) collective-permute-start(f32[1,2,128,128]{3,2,1,0:T(8,128)} %param.7), channel_id=1, source_target_pairs={{0,1},{1,0},{2,3},{3,2},{4,5},{5,4},{6,7},{7,6},{8,9},{9,8},{10,11... | collective-permute-start | bytes 393224 | tf_op jit(solution)/shard_map/ppermute | solution.py:289
  8.3 1.0 %copy-start.1 = (bf16[2,2,256,256]{3,2,1,0:T(8,128)(2,1)S(1)}, bf16[2,2,256,256]{3,2,1,0:T(8,128)(2,1)}, u32[]{:S(2)}) copy-start(bf16[2,2,256,256]{3,2,1,0:T(8,128)(2,1)} %constant.2.clone.table) | copy-start | bytes 1572868
  10.1 0.7 %copy-start.5 = (f32[2,128,256]{2,1,0:T(8,128)}, f32[2,128,256]{2,1,0:T(8,128)S(1)}, u32[]{:S(2)}) copy-start(f32[2,128,256]{2,1,0:T(8,128)S(1)} %get-tuple-element.23) | copy-start | bytes 786436
  10.8 10.1 %collective-permute-start = (f32[2,256,128]{2,1,0:T(8,128)}, f32[2,256,128]{2,1,0:T(8,128)S(1)}, u32[]{:S(2)}, u32[]{:S(2)}) collective-permute-start(f32[2,256,128]{2,1,0:T(8,128)} %get-tuple-element.22), channel_id=1, source_target_pairs={{2,0},{4,2},{6,4},{3,1},{5,3},{7,5},{10,8},{12,10},{14,12},{11,9},... | collective-permute-start | bytes 786440 | tf_op jit(solution)/shard_map/ppermute | solution.py:23
  12.5 11.0 %collective-permute-start.1 = (f32[2,128,256]{2,1,0:T(8,128)}, f32[2,128,256]{2,1,0:T(8,128)S(1)}, u32[]{:S(2)}, u32[]{:S(2)}) collective-permute-start(f32[2,128,256]{2,1,0:T(8,128)} %copy-done.5), channel_id=1, source_target_pairs={{8,0},{16,8},{24,16},{9,1},{17,9},{25,17},{10,2},{18,10},{26,18},{... | collective-permute-start | bytes 786440 | tf_op jit(solution)/shard_map/ppermute | solution.py:23
  15.8 7.7 %copy-start.4 = (f32[1,1,8,128,128]{4,3,2,1,0:T(8,128)S(1)}, f32[1,1,8,128,128]{4,3,2,1,0:T(8,128)}, u32[]{:S(2)}) copy-start(f32[1,1,8,128,128]{4,3,2,1,0:T(8,128)} %param.10) | copy-start | bytes 1572868
  28.7 20.2 %collective-permute-start.6 = (f32[2,128,256]{2,1,0:T(8,128)S(1)}, f32[2,128,256]{2,1,0:T(8,128)S(1)}, u32[]{:S(2)}, u32[]{:S(2)}) collective-permute-start(f32[2,128,256]{2,1,0:T(8,128)S(1)} %get-tuple-element.33), channel_id=1, source_target_pairs={{0,8},{8,16},{16,24},{1,9},{9,17},{17,25},{2,10},{10,18},{18,26},{... | collective-permute-start | bytes 786440 | tf_op jit(solution)/shard_map/ppermute | solution.py:23
  38.3 17.3 %collective-permute-start.7 = (f32[2,2,256,128]{3,2,1,0:T(8,128)S(1)}, f32[2,2,256,128]{3,2,1,0:T(8,128)S(1)}, u32[]{:S(2)}, u32[]{:S(2)}) collective-permute-start(f32[2,2,256,128]{3,2,1,0:T(8,128)S(1)} %get-tuple-element.34), channel_id=1, source_target_pairs={{0,2},{2,4},{4,6},{1,3},{3,5},{5,7},{8,10},{10,12},{12,14},{9,11},... | collective-permute-start | bytes 1572872 | tf_op jit(solution)/shard_map/ppermute | solution.py:23
  40.1 8.9 %collective-permute-start.8 = (f32[2,128,256]{2,1,0:T(8,128)S(1)}, f32[2,128,256]{2,1,0:T(8,128)S(1)}, u32[]{:S(2)}, u32[]{:S(2)}) collective-permute-start(f32[2,128,256]{2,1,0:T(8,128)S(1)} %get-tuple-element.35), channel_id=1, source_target_pairs={{0,8},{8,16},{16,24},{1,9},{9,17},{17,25},{2,10},{10,18},{18,26},{... | collective-permute-start | bytes 786440 | tf_op jit(solution)/shard_map/ppermute | solution.py:23
  44.3 11.3 %collective-permute-start.9 = (f32[2,2,128,128]{3,2,1,0:T(8,128)S(1)}, f32[2,2,128,128]{3,2,1,0:T(8,128)S(1)}, u32[]{:S(2)}, u32[]{:S(2)}) collective-permute-start(f32[2,2,128,128]{3,2,1,0:T(8,128)S(1)} %get-tuple-element.36), channel_id=1, source_target_pairs={{0,10},{2,12},{4,14},{8,18},{10,20},{12,22},{16,26},{18,28},{20,30... | collective-permute-start | bytes 786440 | tf_op jit(solution)/shard_map/ppermute | solution.py:34
where the time goes:
time: 57.8 us; the launch traced here: 56.7 us
  starting transfers between devices  24.7 us (43%)
  Pallas kernels  17.6 us (30%)
  waiting for transfers between devices  11.1 us (19%)
  local copies, waits for them, and re-layouts  3.06 us (5%)
    ppermute x7, starting transfers between devices, passed_along(): return lax.ppermute(value, axis, pairs)  15.9 us
    ppermute x2, waiting for transfers between devices, passed_across(): return lax.ppermute(value, ('row', 'col'), pairs)  6.62 us
    ppermute x2, starting transfers between devices, passed_across(): return lax.ppermute(value, ('row', 'col'), pairs)  5.81 us
    pallas_call x1, Pallas kernels, on_device(): pl.pallas_call(second_kernel, out_shape=(waves, shape(2, t, t), shape(2,...  5.19 us
    pallas_call x1, Pallas kernels, on_device(): pl.pallas_call(middle_kernel, out_shape=waves, in_specs=[SMEM] + [VMEM] *...  5.05 us
    pallas_call x1, Pallas kernels, on_device(): pl.pallas_call(first_kernel, out_shape=(shape(2, t, t), rim_right, rim_lo...  4.86 us
    ppermute x7, waiting for transfers between devices, passed_along(): return lax.ppermute(value, axis, pairs)  4.19 us
    ppermute x1, starting transfers between devices, on_device(): lax.ppermute(probes, 'mode', [(i, (i + by) % mode_count) for i in range(m...  3 us
  transfers between devices with their start and end apart: 10, of which 4 were waited for; matrix products, arithmetic and copies ran while one was open for 0% of the time, Pallas kernels for 20%

commit v1 on v0

--- a/solution.py
+++ b/solution.py
@@ -160,27 +160,34 @@
     corner[...] = total[:, t:, t:]
 
 
-def pack_kernel(objects, tile, lower0, corner, right0):
+def pack_kernel(objects, tile, lower0, corner, right0, sems):
     n = corner.shape[-1]
-    lower0[...] = objects[0, :, :n, :]
-    corner[...] = objects[:, :, :n, :n]
-    right0[...] = objects[0, :, :, :n]
-    tile[...] = objects[...]
-
-
-def stage_kernel(tile, table, lower1, right1, table_out):
-    n = right1.shape[-1]
-    lower1[...] = tile[1, :, :n, :]
-    right1[...] = tile[1, :, :, :n]
+    pieces = (
+        (objects.at[:, :, pl.ds(0, n), pl.ds(0, n)], corner),
+        (objects.at[0, :, pl.ds(0, n), :], lower0),
+        (objects.at[0, :, :, pl.ds(0, n)], right0),
+        (objects, tile),
+    )
+    copies = [pltpu.make_async_copy(piece, out, sems.at[i]) for i, (piece, out) in enumerate(pieces)]
+    for copy in copies:
+        copy.start()
+    for copy in copies:
+        copy.wait()
+
+
+def stage_kernel(tile, lower1):
+    lower1[...] = tile[1, :, : lower1.shape[-2], :]
+
+
+def factor_kernel(*refs):
+    tile, phase, table, out, table_out, right1 = refs[-6:]
+    probes = refs[:-6]
+    for m, probe in enumerate(probes):
+        out[m] = probe[...]
+    out[len(probes), 0] = jnp.cos(phase[...])
+    out[len(probes), 1] = jnp.sin(phase[...])
     table_out[...] = table[...]
-
-
-def factor_kernel(*refs):
-    phase, out = refs[-2:]
-    for m, probe in enumerate(refs[:-2]):
-        out[m] = probe[...]
-    out[len(refs) - 2, 0] = jnp.cos(phase[...])
-    out[len(refs) - 2, 1] = jnp.sin(phase[...])
+    right1[...] = tile[1, :, :, : right1.shape[-1]]
 
 
 def factors_of(factors):
@@ -249,14 +256,17 @@
     out[:, :n] = own[:, :n] + lower[...]
 
 
-def combine_kernel(own0, own1, right, lower0, corner, out):
+def add_right_kernel(own0, own1, right, out):
+    n = right.shape[-1]
+    for s, own in enumerate((own0, own1)):
+        out[s, :, :, n:] = own[:, :, n:]
+        out[s, :, :, :n] = own[:, :, :n] + right[s]
+
+
+def add_corner_kernel(own, corner, out):
     n = corner.shape[-1]
-    out[0] = own0[...]
-    out[1] = own1[...]
-    out[0, :, :n, :] += lower0[...]
-    for s in range(out.shape[0]):
-        out[s, :, :, :n] += right[s]
-        out[s, :, :n, :n] += corner[s]
+    out[...] = own[...]
+    out[:, :, :n, :n] += corner[...]
 
 
 def cost(transforms, n):
@@ -271,15 +281,17 @@
     starts, targets = offsets[0, 0], measured[0, 0]
     count = starts.shape[0]
     shape = lambda *dims: jax.ShapeDtypeStruct(dims, F32)
-    params = pltpu.CompilerParams(vmem_limit_bytes=40 << 20)
+    params = pltpu.CompilerParams(vmem_limit_bytes=24 << 20)
+    small = pltpu.CompilerParams(vmem_limit_bytes=8 << 20)
     rim_right, rim_lower, rim_corner = shape(slices, 2, t, n), shape(2, n, t), shape(slices, 2, n, n)
 
     tile, lower0, corner, right0 = pl.pallas_call(
         pack_kernel,
         out_shape=(shape(*objects.shape), rim_lower, rim_corner, shape(2, t, n)),
-        in_specs=[VMEM],
+        in_specs=[pl.BlockSpec(memory_space=pltpu.HBM)],
         out_specs=(VMEM,) * 4,
-        compiler_params=params,
+        scratch_shapes=[pltpu.SemaphoreType.DMA((4,))],
+        compiler_params=small,
     )(objects)
     lower0 = passed_along(lower0, "row", -1)
     corner = passed_across(corner, -1)
@@ -288,23 +300,23 @@
     for by in range(1, mode_count):
         received.append(lax.ppermute(probes, "mode", [(i, (i + by) % mode_count) for i in range(mode_count)])[0])
 
+    lower1 = pl.pallas_call(
+        stage_kernel, out_shape=rim_lower, in_specs=[VMEM], out_specs=VMEM, compiler_params=small
+    )(tile)
+    lower1 = passed_along(lower1, "row", -1)
     table = tables(n)
-    lower1, right1, table = pl.pallas_call(
-        stage_kernel,
-        out_shape=(rim_lower, shape(2, t, n), jax.ShapeDtypeStruct(table.shape, table.dtype)),
-        in_specs=[VMEM] * 2,
+    factors, table, right1 = pl.pallas_call(
+        factor_kernel,
+        out_shape=(
+            shape(mode_count + 1, 2, n, n),
+            jax.ShapeDtypeStruct(table.shape, table.dtype),
+            shape(2, t, n),
+        ),
+        in_specs=[VMEM] * (mode_count + 3),
         out_specs=(VMEM,) * 3,
-        compiler_params=params,
-    )(tile, table)
-    lower1 = passed_along(lower1, "row", -1)
+        compiler_params=small,
+    )(probes[0], *received, tile, phase, table)
     right1 = passed_along(right1, "col", -1)
-    factors = pl.pallas_call(
-        factor_kernel,
-        out_shape=shape(mode_count + 1, 2, n, n),
-        in_specs=[VMEM] * (mode_count + 1),
-        out_specs=VMEM,
-        compiler_params=params,
-    )(probes[0], *received, phase)
     waves = shape(count, mode_count, 2, n, n)
     window_area = pltpu.VMEM((2, reach, reach), F32)
     middle = pl.pallas_call(
@@ -317,7 +329,7 @@
         cost_estimate=cost(12 * count * mode_count, n),
     )(starts, tile, right0, lower0, corner, factors, table)
 
-    back, own1, grad_right, grad_lower1, grad_corner = pl.pallas_call(
+    back, own1, grad_right1, grad_lower1, grad_corner1 = pl.pallas_call(
         second_kernel,
         out_shape=(waves, shape(2, t, t), shape(2, t, n), rim_lower, shape(2, n, n)),
         in_specs=[SMEM] + [VMEM] * 7,
@@ -327,7 +339,6 @@
         cost_estimate=cost(6 * count * mode_count, n),
     )(starts, tile, right1, lower1, corner, middle, targets, table)
     grad_lower1 = passed_along(grad_lower1, "row", 1)
-
     own0, grad_right, grad_lower0, grad_corner = pl.pallas_call(
         first_kernel,
         out_shape=(shape(2, t, t), rim_right, rim_lower, rim_corner),
@@ -336,27 +347,39 @@
         scratch_shapes=[window_area],
         compiler_params=params,
         cost_estimate=cost(6 * count * mode_count, n),
-    )(starts, back, factors, table, grad_right, grad_corner)
+    )(starts, back, factors, table, grad_right1, grad_corner1)
     grad_lower0 = passed_along(grad_lower0, "row", 1)
     grad_right = passed_along(grad_right, "col", 1)
     grad_corner = passed_across(grad_corner, 1)
 
-    own1 = pl.pallas_call(
-        add_lower_kernel,
-        out_shape=shape(2, t, t),
+    def with_lower(own, lower, weight):
+        return pl.pallas_call(
+            add_lower_kernel,
+            out_shape=shape(2, t, t),
+            in_specs=[VMEM] * 2,
+            out_specs=VMEM,
+            input_output_aliases={0: 0},
+            compiler_params=small,
+            cost_estimate=cost(weight, n),
+        )(own, lower)
+
+    own1 = with_lower(own1, grad_lower1, 20)
+    own0 = with_lower(own0, grad_lower0, 90)
+    own = pl.pallas_call(
+        add_right_kernel,
+        out_shape=shape(*objects.shape),
+        in_specs=[VMEM] * 3,
+        out_specs=VMEM,
+        compiler_params=small,
+        cost_estimate=cost(0, n),
+    )(own0, own1, grad_right)
+    return pl.pallas_call(
+        add_corner_kernel,
+        out_shape=shape(*objects.shape),
         in_specs=[VMEM] * 2,
         out_specs=VMEM,
-        input_output_aliases={0: 0},
-        compiler_params=params,
-        cost_estimate=cost(64, n),
-    )(own1, grad_lower1)
-    return pl.pallas_call(
-        combine_kernel,
-        out_shape=jax.ShapeDtypeStruct(objects.shape, F32),
-        in_specs=[VMEM] * 5,
-        out_specs=VMEM,
-        compiler_params=params,
-    )(own0, own1, grad_right, grad_lower0, grad_corner)
+        compiler_params=small,
+    )(own, grad_corner)
 
 
 def solution(mesh):

time: 57.8 us -> 55.5 us (0.960); the launches traced: 56.7 us -> 55.1 us
  local copies, waits for them, and re-layouts: 3.06 us -> 1.32 us
  waiting for transfers between devices: 11.1 us -> 10.2 us
  Pallas kernels: 17.6 us -> 18.2 us
    ppermute x1, waiting for transfers between devices: 0.31 us -> 2.79 us  [on_device(): lax.ppermute(probes, 'mode', [(i, (i + by) % mode_count) for i in range(m...]
    ppermute x7, waiting for transfers between devices: 4.19 us -> 1.89 us  [passed_along(): return lax.ppermute(value, axis, pairs)]
    unnamed x14 -> x12, local copies, waits for them, and re-layouts: 2.98 us -> 1.24 us
    ppermute x2, waiting for transfers between devices: 6.62 us -> 5.5 us  [passed_across(): return lax.ppermute(value, ('row', 'col'), pairs)]
    ppermute x2, starting transfers between devices: 5.81 us -> 6.77 us  [passed_across(): return lax.ppermute(value, ('row', 'col'), pairs)]
    pallas_call x1, Pallas kernels: 0.12 us -> 0.87 us  [on_device(): pl.pallas_call(pack_kernel, out_shape=(shape(*objects.shape), rim_lower,...]
    pallas_call x4 -> x6, Pallas kernels: 2.41 us -> 1.79 us  [the longest x1 1.05 us: on_device(): pl.pallas_call(add_corner_kernel, out_shape=shape(*objects.shape), in_spe...]
where the time goes in v1:
time: 55.5 us; the launch traced here: 55.1 us
  starting transfers between devices  25.2 us (45%)
  Pallas kernels  18.2 us (33%)
  waiting for transfers between devices  10.2 us (18%)
  local copies, waits for them, and re-layouts  1.32 us (2%)
    ppermute x7, starting transfers between devices, passed_along(): return lax.ppermute(value, axis, pairs)  15.4 us
    ppermute x2, starting transfers between devices, passed_across(): return lax.ppermute(value, ('row', 'col'), pairs)  6.77 us
    ppermute x2, waiting for transfers between devices, passed_across(): return lax.ppermute(value, ('row', 'col'), pairs)  5.5 us
    pallas_call x1, Pallas kernels, on_device(): pl.pallas_call(second_kernel, out_shape=(waves, shape(2, t, t), shape(2,...  5.43 us
    pallas_call x1, Pallas kernels, on_device(): pl.pallas_call(middle_kernel, out_shape=waves, in_specs=[SMEM] + [VMEM] *...  5.16 us
    pallas_call x1, Pallas kernels, on_device(): pl.pallas_call(first_kernel, out_shape=(shape(2, t, t), rim_right, rim_lo...  4.98 us
    ppermute x1, starting transfers between devices, on_device(): lax.ppermute(probes, 'mode', [(i, (i + by) % mode_count) for i in range(m...  3 us
    ppermute x1, waiting for transfers between devices, on_device(): lax.ppermute(probes, 'mode', [(i, (i + by) % mode_count) for i in range(m...  2.79 us
  transfers between devices with their start and end apart: 10, of which 4 were waited for; matrix products, arithmetic and copies ran while one was open for 0% of the time, Pallas kernels for 20%

profile of v1, /device:TPU:0, one launch (start us, length us, event | category | flops | bytes accessed | tf_op | source)
XLA Modules:
  0.0 55.1 jit_solution(9313614257071904457)
XLA Ops:
  0.0 0.0 copy-start
  0.0 1.2 %copy-done = f32[2,2,256,256]{3,2,1,0:T(8,128)S(1)} copy-done((f32[2,2,256,256]{3,2,1,0:T(8,128)S(1)}, f32[2,2,256,256]{3,2,1,0:T(8,128)}, u32[]{:S(2)}) %copy-start) | copy-done | bytes 1048600
  1.2 0.0 copy-start.5
  1.2 0.0 copy-start.1
  1.2 0.0 copy-start.2
  1.2 0.0 copy-start.3
  1.2 0.9 %shard_map.64 = (f32[2,2,256,256]{3,2,1,0:T(8,128)S(1)}, f32[2,128,256]{2,1,0:T(8,128)S(1)}, f32[2,2,128,128]{3,2,1,0:T(8,128)}, f32[2,256,128]{2,1,0:T(8,128)S(1)}) custom-call(f32[2,2,256,256]{3,2,1,0:T(8,128)S(1)} %copy-done), custom_call_target="tpu_custom_call" | custom-call | tf_op jit(solution)/shard_map/pallas_call | solution.py:288
  2.1 1.3 %collective-permute-start.3 = (f32[2,2,128,128]{3,2,1,0:T(8,128)}, f32[2,2,128,128]{3,2,1,0:T(8,128)S(1)}, u32[]{:S(2)}, u32[]{:S(2)}) collective-permute-start(f32[2,2,128,128]{3,2,1,0:T(8,128)} %get-tuple-element.23), channel_id=1, source_target_pairs={{10,0},{12,2},{14,4},{18,8},{20,10},{22,12},{26,16},{28,18},{30,20... | collective-permute-start | bytes 786440 | tf_op jit(solution)/shard_map/ppermute | solution.py:34
  3.4 1.3 %collective-permute-start.4 = (f32[2,256,128]{2,1,0:T(8,128)S(1)}, f32[2,256,128]{2,1,0:T(8,128)S(1)}, u32[]{:S(2)}, u32[]{:S(2)}) collective-permute-start(f32[2,256,128]{2,1,0:T(8,128)S(1)} %get-tuple-element.24), channel_id=1, source_target_pairs={{2,0},{4,2},{6,4},{3,1},{5,3},{7,5},{10,8},{12,10},{14,12},{11,9},... | collective-permute-start | bytes 786440 | tf_op jit(solution)/shard_map/ppermute | solution.py:23
  4.7 1.3 %collective-permute-start.5 = (f32[2,128,256]{2,1,0:T(8,128)S(1)}, f32[2,128,256]{2,1,0:T(8,128)}, u32[]{:S(2)}, u32[]{:S(2)}) collective-permute-start(f32[2,128,256]{2,1,0:T(8,128)S(1)} %get-tuple-element.25), channel_id=1, source_target_pairs={{8,0},{16,8},{24,16},{9,1},{17,9},{25,17},{10,2},{18,10},{26,18},{... | collective-permute-start | bytes 786440 | tf_op jit(solution)/shard_map/ppermute | solution.py:23
  6.0 3.0 %collective-permute-start = (f32[1,2,128,128]{3,2,1,0:T(8,128)}, f32[1,2,128,128]{3,2,1,0:T(8,128)S(1)}, u32[]{:S(2)}, u32[]{:S(2)}) collective-permute-start(f32[1,2,128,128]{3,2,1,0:T(8,128)} %param.7), channel_id=1, source_target_pairs={{0,1},{1,0},{2,3},{3,2},{4,5},{5,4},{6,7},{7,6},{8,9},{9,8},{10,11... | collective-permute-start | bytes 393224 | tf_op jit(solution)/shard_map/ppermute | solution.py:301
  9.0 1.3 %collective-permute-start.2 = (f32[2,128,256]{2,1,0:T(8,128)S(1)}, f32[2,128,256]{2,1,0:T(8,128)S(1)}, u32[]{:S(2)}, u32[]{:S(2)}) collective-permute-start(f32[2,128,256]{2,1,0:T(8,128)S(1)} %shard_map.66), channel_id=1, source_target_pairs={{8,0},{16,8},{24,16},{9,1},{17,9},{25,17},{10,2},{18,10},{26,18},{... | collective-permute-start | bytes 786440 | tf_op jit(solution)/shard_map/ppermute | solution.py:23
  10.3 0.0 copy-done.5
  10.4 0.1 copy.11.offsets
  10.4 2.8 %collective-permute-done = f32[1,2,128,128]{3,2,1,0:T(8,128)S(1)} collective-permute-done((f32[1,2,128,128]{3,2,1,0:T(8,128)}, f32[1,2,128,128]{3,2,1,0:T(8,128)S(1)}, u32[]{:S(2)}, u32[]{:S(2)}) %collective-permute-start) | collective-permute-done | bytes 131104 | tf_op jit(solution)/shard_map/ppermute | solution.py:301
  13.2 0.0 copy-done.1
  13.2 0.0 copy-done.2
  13.2 0.0 copy-done.3
  13.2 0.5 shard_map.65
  13.7 1.3 %collective-permute-start.1 = (f32[2,256,128]{2,1,0:T(8,128)S(1)}, f32[2,256,128]{2,1,0:T(8,128)S(1)}, u32[]{:S(2)}, u32[]{:S(2)}) collective-permute-start(f32[2,256,128]{2,1,0:T(8,128)S(1)} %get-tuple-element.22), channel_id=1, source_target_pairs={{2,0},{4,2},{6,4},{3,1},{5,3},{7,5},{10,8},{12,10},{14,12},{11,9},... | collective-permute-start | bytes 786440 | tf_op jit(solution)/shard_map/ppermute | solution.py:23
  15.0 0.0 collective-permute-done.3.corner
  15.0 0.0 collective-permute-done.4.right
  15.0 1.5 %collective-permute-done.5.lower = f32[2,128,256]{2,1,0:T(8,128)} collective-permute-done((f32[2,128,256]{2,1,0:T(8,128)S(1)}, f32[2,128,256]{2,1,0:T(8,128)}, u32[]{:S(2)}, u32[]{:S(2)}) %collective-permute-start.5) | collective-permute-done | bytes 262176 | tf_op jit(solution)/shard_map/ppermute | solution.py:23
  16.6 0.0 copy-start.4
  16.6 5.2 %shard_map.67.middle = f32[8,2,2,128,128]{4,3,2,1,0:T(8,128)S(1)} custom-call(s32[8,2]{1,0:T(8,128)S(1)} %copy.11.offsets, f32[2,2,256,256]{3,2,1,0:T(8,128)S(1)} %get-tuple-element.21.refs_2_.tile.objects, f32[2,256,128]{2,1,0:T(8,128)S(1)} %collective-permute-done.4.right, f32[2,128,256]{2,1,0:T(8,128)} %collective-permute-done.5.lower, ...), custom_call_target="tpu_custom_call" | custom-call | flops 9663676416 | bytes 4194304 | tf_op jit(solution)/shard_map/pallas_call | solution.py:322
  21.7 0.3 collective-permute-done.2.lower
  22.1 0.0 collective-permute-done.1.right
  22.1 0.0 copy-done.4
  22.1 5.4 %shard_map.68 = (f32[8,2,2,128,128]{4,3,2,1,0:T(8,128)S(1)}, f32[2,256,256]{2,1,0:T(8,128)S(1)}, f32[2,256,128]{2,1,0:T(8,128)S(1)}, f32[2,128,256]{2,1,0:T(8,128)S(1)}, f32[2,128,128]{2,1,0:T(8,128)S(1)}) custom-call(s32[8,2]{1,0:T(8,128)S(1)} %copy.11.offsets, f32[2,2,256,256]{3,2,1,0:T(8,128)S(1)} %get-tuple-element.21.refs_2_.tile.objects, ...), custom_call_target="tpu_custom_call" | custom-call | flops 4831838208 | bytes 4194304 | tf_op jit(solution)/shard_map/pallas_call | solution.py:332
  27.5 3.9 %collective-permute-start.7 = (f32[2,128,256]{2,1,0:T(8,128)S(1)}, f32[2,128,256]{2,1,0:T(8,128)S(1)}, u32[]{:S(2)}, u32[]{:S(2)}) collective-permute-start(f32[2,128,256]{2,1,0:T(8,128)S(1)} %get-tuple-element.34), channel_id=1, source_target_pairs={{0,8},{8,16},{16,24},{1,9},{9,17},{17,25},{2,10},{10,18},{18,26},{... | collective-permute-start | bytes 786440 | tf_op jit(solution)/shard_map/ppermute | solution.py:23
  31.4 5.0 %shard_map.69 = (f32[2,256,256]{2,1,0:T(8,128)S(1)}, f32[2,2,256,128]{3,2,1,0:T(8,128)S(1)}, f32[2,128,256]{2,1,0:T(8,128)S(1)}, f32[2,2,128,128]{3,2,1,0:T(8,128)S(1)}) custom-call(s32[8,2]{1,0:T(8,128)S(1)} %copy.11.offsets, f32[8,2,2,128,128]{4,3,2,1,0:T(8,128)S(1)} %get-tuple-element.28.back, f32[3,2,128,128]{3,2,1,0:T(8,128)S(1)} %get-tuple-element.26.factors, ...), custom_call_target="tpu_custom_call" | custom-call | flops 4831838208 | bytes 4194304 | tf_op jit(solution)/shard_map/pallas_call | solution.py:342
  36.4 3.3 %collective-permute-start.6 = (f32[2,128,256]{2,1,0:T(8,128)S(1)}, f32[2,128,256]{2,1,0:T(8,128)S(1)}, u32[]{:S(2)}, u32[]{:S(2)}) collective-permute-start(f32[2,128,256]{2,1,0:T(8,128)S(1)} %get-tuple-element.32), channel_id=1, source_target_pairs={{0,8},{8,16},{16,24},{1,9},{9,17},{17,25},{2,10},{10,18},{18,26},{... | collective-permute-start | bytes 786440 | tf_op jit(solution)/shard_map/ppermute | solution.py:23
  39.7 3.1 %collective-permute-start.8 = (f32[2,2,256,128]{3,2,1,0:T(8,128)S(1)}, f32[2,2,256,128]{3,2,1,0:T(8,128)S(1)}, u32[]{:S(2)}, u32[]{:S(2)}) collective-permute-start(f32[2,2,256,128]{3,2,1,0:T(8,128)S(1)} %get-tuple-element.35), channel_id=1, source_target_pairs={{0,2},{2,4},{4,6},{1,3},{3,5},{5,7},{8,10},{10,12},{12,14},{9,11},... | collective-permute-start | bytes 1572872 | tf_op jit(solution)/shard_map/ppermute | solution.py:23
  42.8 5.5 %collective-permute-start.9 = (f32[2,2,128,128]{3,2,1,0:T(8,128)S(1)}, f32[2,2,128,128]{3,2,1,0:T(8,128)S(1)}, u32[]{:S(2)}, u32[]{:S(2)}) collective-permute-start(f32[2,2,128,128]{3,2,1,0:T(8,128)S(1)} %get-tuple-element.36), channel_id=1, source_target_pairs={{0,10},{2,12},{4,14},{8,18},{10,20},{12,22},{16,26},{18,28},{20,30... | collective-permute-start | bytes 786440 | tf_op jit(solution)/shard_map/ppermute | solution.py:34
  48.2 0.0 collective-permute-done.7.lower
  48.2 0.1 shard_map.71.own1
  48.3 0.0 collective-permute-done.6.lower
  48.3 0.1 shard_map.70.own0
  48.4 0.0 collective-permute-done.8.right
  48.4 0.1 shard_map.72.own
  48.6 5.5 %collective-permute-done.9.corner = f32[2,2,128,128]{3,2,1,0:T(8,128)S(1)} collective-permute-done((f32[2,2,128,128]{3,2,1,0:T(8,128)S(1)}, f32[2,2,128,128]{3,2,1,0:T(8,128)S(1)}, u32[]{:S(2)}, u32[]{:S(2)}) %collective-permute-start.9) | collective-permute-done | bytes 262176 | tf_op jit(solution)/shard_map/ppermute | solution.py:34
  54.1 1.0 %shard_map.73 = f32[2,2,256,256]{3,2,1,0:T(8,128)} custom-call(f32[2,2,256,256]{3,2,1,0:T(8,128)S(1)} %shard_map.72.own, f32[2,2,128,128]{3,2,1,0:T(8,128)S(1)} %collective-permute-done.9.corner), custom_call_target="tpu_custom_call" | custom-call | tf_op jit(solution)/shard_map/pallas_call | solution.py:376
  (1 shorter events, 0.0 us)
Async XLA Ops:
  0.0 1.2 %copy-start = (f32[2,2,256,256]{3,2,1,0:T(8,128)S(1)}, f32[2,2,256,256]{3,2,1,0:T(8,128)}, u32[]{:S(2)}) copy-start(f32[2,2,256,256]{3,2,1,0:T(8,128)} %objects.1) | copy-start | bytes 3145732
  1.2 9.1 %copy-start.5 = (s32[1,1,8,2]{2,3,1,0:T(2,128)S(1)}, s32[1,1,8,2]{2,3,1,0:T(2,128)}, u32[]{:S(2)}) copy-start(s32[1,1,8,2]{2,3,1,0:T(2,128)} %param.9) | copy-start | bytes 196
  1.2 12.0 %copy-start.1 = (bf16[2,2,256,256]{3,2,1,0:T(8,128)(2,1)S(1)}, bf16[2,2,256,256]{3,2,1,0:T(8,128)(2,1)}, u32[]{:S(2)}) copy-start(bf16[2,2,256,256]{3,2,1,0:T(8,128)(2,1)} %constant.2.clone.refs_4_) | copy-start | bytes 1572868
  1.2 12.0 %copy-start.2 = (f32[1,2,128,128]{3,2,1,0:T(8,128)S(1)}, f32[1,2,128,128]{3,2,1,0:T(8,128)}, u32[]{:S(2)}) copy-start(f32[1,2,128,128]{3,2,1,0:T(8,128)} %param.7) | copy-start | bytes 393220
  1.2 12.0 %copy-start.3 = (f32[128,128]{1,0:T(8,128)S(1)}, f32[128,128]{1,0:T(8,128)}, u32[]{:S(2)}) copy-start(f32[128,128]{1,0:T(8,128)} %refs_3_.1) | copy-start | bytes 196612
  2.1 12.9 %collective-permute-start.3 = (f32[2,2,128,128]{3,2,1,0:T(8,128)}, f32[2,2,128,128]{3,2,1,0:T(8,128)S(1)}, u32[]{:S(2)}, u32[]{:S(2)}) collective-permute-start(f32[2,2,128,128]{3,2,1,0:T(8,128)} %get-tuple-element.23), channel_id=1, source_target_pairs={{10,0},{12,2},{14,4},{18,8},{20,10},{22,12},{26,16},{28,18},{30,20... | collective-permute-start | bytes 786440 | tf_op jit(solution)/shard_map/ppermute | solution.py:34
  3.4 11.6 %collective-permute-start.4 = (f32[2,256,128]{2,1,0:T(8,128)S(1)}, f32[2,256,128]{2,1,0:T(8,128)S(1)}, u32[]{:S(2)}, u32[]{:S(2)}) collective-permute-start(f32[2,256,128]{2,1,0:T(8,128)S(1)} %get-tuple-element.24), channel_id=1, source_target_pairs={{2,0},{4,2},{6,4},{3,1},{5,3},{7,5},{10,8},{12,10},{14,12},{11,9},... | collective-permute-start | bytes 786440 | tf_op jit(solution)/shard_map/ppermute | solution.py:23
  4.7 11.8 %collective-permute-start.5 = (f32[2,128,256]{2,1,0:T(8,128)S(1)}, f32[2,128,256]{2,1,0:T(8,128)}, u32[]{:S(2)}, u32[]{:S(2)}) collective-permute-start(f32[2,128,256]{2,1,0:T(8,128)S(1)} %get-tuple-element.25), channel_id=1, source_target_pairs={{8,0},{16,8},{24,16},{9,1},{17,9},{25,17},{10,2},{18,10},{26,18},{... | collective-permute-start | bytes 786440 | tf_op jit(solution)/shard_map/ppermute | solution.py:23
  6.0 7.2 %collective-permute-start = (f32[1,2,128,128]{3,2,1,0:T(8,128)}, f32[1,2,128,128]{3,2,1,0:T(8,128)S(1)}, u32[]{:S(2)}, u32[]{:S(2)}) collective-permute-start(f32[1,2,128,128]{3,2,1,0:T(8,128)} %param.7), channel_id=1, source_target_pairs={{0,1},{1,0},{2,3},{3,2},{4,5},{5,4},{6,7},{7,6},{8,9},{9,8},{10,11... | collective-permute-start | bytes 393224 | tf_op jit(solution)/shard_map/ppermute | solution.py:301
  9.0 13.0 %collective-permute-start.2 = (f32[2,128,256]{2,1,0:T(8,128)S(1)}, f32[2,128,256]{2,1,0:T(8,128)S(1)}, u32[]{:S(2)}, u32[]{:S(2)}) collective-permute-start(f32[2,128,256]{2,1,0:T(8,128)S(1)} %shard_map.66), channel_id=1, source_target_pairs={{8,0},{16,8},{24,16},{9,1},{17,9},{25,17},{10,2},{18,10},{26,18},{... | collective-permute-start | bytes 786440 | tf_op jit(solution)/shard_map/ppermute | solution.py:23
  13.7 8.4 %collective-permute-start.1 = (f32[2,256,128]{2,1,0:T(8,128)S(1)}, f32[2,256,128]{2,1,0:T(8,128)S(1)}, u32[]{:S(2)}, u32[]{:S(2)}) collective-permute-start(f32[2,256,128]{2,1,0:T(8,128)S(1)} %get-tuple-element.22), channel_id=1, source_target_pairs={{2,0},{4,2},{6,4},{3,1},{5,3},{7,5},{10,8},{12,10},{14,12},{11,9},... | collective-permute-start | bytes 786440 | tf_op jit(solution)/shard_map/ppermute | solution.py:23
  16.6 5.5 %copy-start.4 = (f32[1,1,8,128,128]{4,3,2,1,0:T(8,128)S(1)}, f32[1,1,8,128,128]{4,3,2,1,0:T(8,128)}, u32[]{:S(2)}) copy-start(f32[1,1,8,128,128]{4,3,2,1,0:T(8,128)} %param.10) | copy-start | bytes 1572868
  27.5 20.7 %collective-permute-start.7 = (f32[2,128,256]{2,1,0:T(8,128)S(1)}, f32[2,128,256]{2,1,0:T(8,128)S(1)}, u32[]{:S(2)}, u32[]{:S(2)}) collective-permute-start(f32[2,128,256]{2,1,0:T(8,128)S(1)} %get-tuple-element.34), channel_id=1, source_target_pairs={{0,8},{8,16},{16,24},{1,9},{9,17},{17,25},{2,10},{10,18},{18,26},{... | collective-permute-start | bytes 786440 | tf_op jit(solution)/shard_map/ppermute | solution.py:23
  36.4 12.0 %collective-permute-start.6 = (f32[2,128,256]{2,1,0:T(8,128)S(1)}, f32[2,128,256]{2,1,0:T(8,128)S(1)}, u32[]{:S(2)}, u32[]{:S(2)}) collective-permute-start(f32[2,128,256]{2,1,0:T(8,128)S(1)} %get-tuple-element.32), channel_id=1, source_target_pairs={{0,8},{8,16},{16,24},{1,9},{9,17},{17,25},{2,10},{10,18},{18,26},{... | collective-permute-start | bytes 786440 | tf_op jit(solution)/shard_map/ppermute | solution.py:23
  39.7 8.8 %collective-permute-start.8 = (f32[2,2,256,128]{3,2,1,0:T(8,128)S(1)}, f32[2,2,256,128]{3,2,1,0:T(8,128)S(1)}, u32[]{:S(2)}, u32[]{:S(2)}) collective-permute-start(f32[2,2,256,128]{3,2,1,0:T(8,128)S(1)} %get-tuple-element.35), channel_id=1, source_target_pairs={{0,2},{2,4},{4,6},{1,3},{3,5},{5,7},{8,10},{10,12},{12,14},{9,11},... | collective-permute-start | bytes 1572872 | tf_op jit(solution)/shard_map/ppermute | solution.py:23
  42.8 11.3 %collective-permute-start.9 = (f32[2,2,128,128]{3,2,1,0:T(8,128)S(1)}, f32[2,2,128,128]{3,2,1,0:T(8,128)S(1)}, u32[]{:S(2)}, u32[]{:S(2)}) collective-permute-start(f32[2,2,128,128]{3,2,1,0:T(8,128)S(1)} %get-tuple-element.36), channel_id=1, source_target_pairs={{0,10},{2,12},{4,14},{8,18},{10,20},{12,22},{16,26},{18,28},{20,30... | collective-permute-start | bytes 786440 | tf_op jit(solution)/shard_map/ppermute | solution.py:34

commit v2 on v1

--- a/solution.py
+++ b/solution.py
@@ -127,7 +127,7 @@
 
 def deposit_pair(target, place, terms):
     for channel in range(2):
-        deposit(target, channel, place, summed([term[channel] for term in terms]))
+        deposit(target[channel], 0, place, summed([term[channel] for term in terms]))
 
 
 def keep(target, position, modes):
@@ -154,10 +154,11 @@
 
 def part_ways(total, own, right, lower, corner):
     t = own.shape[-1]
-    own[...] = total[:, :t, :t]
-    right[...] = total[:, :t, t:]
-    lower[...] = total[:, t:, :t]
-    corner[...] = total[:, t:, t:]
+    for channel, plane in enumerate(total):
+        own[channel] = plane[0, :t, :t]
+        right[channel] = plane[0, :t, t:]
+        lower[channel] = plane[0, t:, :t]
+        corner[channel] = plane[0, t:, t:]
 
 
 def pack_kernel(objects, tile, lower0, corner, right0, sems):
@@ -211,11 +212,12 @@
 
 def second_kernel(
     offsets, objects, right, lower, corner, middle, measured, table,
-    back, own, rim_right, rim_lower, rim_corner, extended, total,
+    back, own, rim_right, rim_lower, rim_corner, extended, *total,
 ):
     n = corner.shape[-1]
     join(extended, objects.at[1], right, lower, corner.at[1])
-    total[...] = jnp.zeros_like(total)
+    for plane in total:
+        plane[...] = jnp.zeros_like(plane)
     for group in groups_of(offsets.shape[0]):
         windows = [cut_pair(extended, place_of(offsets, k, n), n) for k in group]
         waves = [kept(middle, k) for k in group]
@@ -234,11 +236,12 @@
 
 
 def first_kernel(
-    offsets, back, factors, table, other_right, other_corner, own, rim_right, rim_lower, rim_corner, total
+    offsets, back, factors, table, other_right, other_corner, own, rim_right, rim_lower, rim_corner, *total
 ):
     n = rim_corner.shape[-1]
     probes, spread = factors_of(factors)
-    total[...] = jnp.zeros_like(total)
+    for plane in total:
+        plane[...] = jnp.zeros_like(plane)
     rim_right[1] = other_right[...]
     rim_corner[1] = other_corner[...]
     for group in groups_of(offsets.shape[0]):
@@ -256,17 +259,19 @@
     out[:, :n] = own[:, :n] + lower[...]
 
 
-def add_right_kernel(own0, own1, right, out):
+def write_kernel(own0, own1, out):
+    out[0] = own0[...]
+    out[1] = own1[...]
+
+
+def finish_kernel(written, own0, own1, right, corner, out, left, sem):
     n = right.shape[-1]
     for s, own in enumerate((own0, own1)):
-        out[s, :, :, n:] = own[:, :, n:]
-        out[s, :, :, :n] = own[:, :, :n] + right[s]
-
-
-def add_corner_kernel(own, corner, out):
-    n = corner.shape[-1]
-    out[...] = own[...]
-    out[:, :, :n, :n] += corner[...]
+        left[s] = own[:, :, :n] + right[s]
+    left[:, :, :n, :] += corner[...]
+    copy = pltpu.make_async_copy(left, out.at[:, :, :, pl.ds(0, n)], sem)
+    copy.start()
+    copy.wait()
 
 
 def cost(transforms, n):
@@ -319,6 +324,7 @@
     right1 = passed_along(right1, "col", -1)
     waves = shape(count, mode_count, 2, n, n)
     window_area = pltpu.VMEM((2, reach, reach), F32)
+    planes = [pltpu.VMEM((1, reach, reach), F32)] * 2
     middle = pl.pallas_call(
         middle_kernel,
         out_shape=waves,
@@ -334,7 +340,7 @@
         out_shape=(waves, shape(2, t, t), shape(2, t, n), rim_lower, shape(2, n, n)),
         in_specs=[SMEM] + [VMEM] * 7,
         out_specs=(VMEM,) * 5,
-        scratch_shapes=[window_area] * 2,
+        scratch_shapes=[window_area, *planes],
         compiler_params=params,
         cost_estimate=cost(6 * count * mode_count, n),
     )(starts, tile, right1, lower1, corner, middle, targets, table)
@@ -344,7 +350,7 @@
         out_shape=(shape(2, t, t), rim_right, rim_lower, rim_corner),
         in_specs=[SMEM] + [VMEM] * 5,
         out_specs=(VMEM,) * 4,
-        scratch_shapes=[window_area],
+        scratch_shapes=planes,
         compiler_params=params,
         cost_estimate=cost(6 * count * mode_count, n),
     )(starts, back, factors, table, grad_right1, grad_corner1)
@@ -365,21 +371,23 @@
 
     own1 = with_lower(own1, grad_lower1, 20)
     own0 = with_lower(own0, grad_lower0, 90)
-    own = pl.pallas_call(
-        add_right_kernel,
-        out_shape=shape(*objects.shape),
-        in_specs=[VMEM] * 3,
-        out_specs=VMEM,
-        compiler_params=small,
-        cost_estimate=cost(0, n),
-    )(own0, own1, grad_right)
-    return pl.pallas_call(
-        add_corner_kernel,
+    written = pl.pallas_call(
+        write_kernel,
         out_shape=shape(*objects.shape),
         in_specs=[VMEM] * 2,
         out_specs=VMEM,
         compiler_params=small,
-    )(own, grad_corner)
+        cost_estimate=cost(0, n),
+    )(own0, own1)
+    return pl.pallas_call(
+        finish_kernel,
+        out_shape=shape(*objects.shape),
+        in_specs=[pl.BlockSpec(memory_space=pl.ANY)] + [VMEM] * 4,
+        out_specs=pl.BlockSpec(memory_space=pl.ANY),
+        scratch_shapes=[pltpu.VMEM((slices, 2, t, n), F32), pltpu.SemaphoreType.DMA],
+        input_output_aliases={0: 0},
+        compiler_params=small,
+    )(written, own0, own1, grad_right, grad_corner)
 
 
 def solution(mesh):

time: 55.5 us -> 55.4 us (level)
  waiting for transfers between devices: 10.2 us -> 9.27 us
  Pallas kernels: 18.2 us -> 19 us
    ppermute x2, waiting for transfers between devices: 5.5 us -> 4.58 us  [passed_across(): return lax.ppermute(value, ('row', 'col'), pairs)]
    pallas_call x2, Pallas kernels: 1.16 us -> 1.94 us  [the longest x1 1.04 us: on_device(): pl.pallas_call(write_kernel, out_shape=shape(*objects.shape), in_specs=[V...]
  transfers between devices with their start and end apart: 10 -> 10, of which waited for: 4 -> 4; matrix products, arithmetic and copies ran while one was open for 0% -> 0% of each run, Pallas kernels for 20% -> 21%
where the time goes in v2:
time: 55.4 us; the launch traced here: 55 us
  starting transfers between devices  25.1 us (45%)
  Pallas kernels  19 us (34%)
  waiting for transfers between devices  9.27 us (17%)
  local copies, waits for them, and re-layouts  1.32 us (2%)
    ppermute x7, starting transfers between devices, passed_along(): return lax.ppermute(value, axis, pairs)  15.4 us
    ppermute x2, starting transfers between devices, passed_across(): return lax.ppermute(value, ('row', 'col'), pairs)  6.7 us
    pallas_call x1, Pallas kernels, on_device(): pl.pallas_call(second_kernel, out_shape=(waves, shape(2, t, t), shape(2,...  5.43 us
    pallas_call x1, Pallas kernels, on_device(): pl.pallas_call(middle_kernel, out_shape=waves, in_specs=[SMEM] + [VMEM] *...  5.15 us
    pallas_call x1, Pallas kernels, on_device(): pl.pallas_call(first_kernel, out_shape=(shape(2, t, t), rim_right, rim_lo...  4.99 us
    ppermute x2, waiting for transfers between devices, passed_across(): return lax.ppermute(value, ('row', 'col'), pairs)  4.58 us
    ppermute x1, starting transfers between devices, on_device(): lax.ppermute(probes, 'mode', [(i, (i + by) % mode_count) for i in range(m...  3 us
    ppermute x1, waiting for transfers between devices, on_device(): lax.ppermute(probes, 'mode', [(i, (i + by) % mode_count) for i in range(m...  2.79 us
  transfers between devices with their start and end apart: 10, of which 4 were waited for; matrix products, arithmetic and copies ran while one was open for 0% of the time, Pallas kernels for 21%

profile of v2, /device:TPU:0, one launch (start us, length us, event | category | flops | bytes accessed | tf_op | source)
XLA Modules:
  0.0 55.0 jit_solution(11715284522177399272)
XLA Ops:
  0.0 0.0 copy-start
  0.0 1.2 %copy-done = f32[2,2,256,256]{3,2,1,0:T(8,128)S(1)} copy-done((f32[2,2,256,256]{3,2,1,0:T(8,128)S(1)}, f32[2,2,256,256]{3,2,1,0:T(8,128)}, u32[]{:S(2)}) %copy-start) | copy-done | bytes 1048600
  1.2 0.0 copy-start.5
  1.2 0.0 copy-start.1
  1.2 0.0 copy-start.2
  1.2 0.0 copy-start.3
  1.2 0.9 %shard_map.64 = (f32[2,2,256,256]{3,2,1,0:T(8,128)S(1)}, f32[2,128,256]{2,1,0:T(8,128)S(1)}, f32[2,2,128,128]{3,2,1,0:T(8,128)}, f32[2,256,128]{2,1,0:T(8,128)S(1)}) custom-call(f32[2,2,256,256]{3,2,1,0:T(8,128)S(1)} %copy-done), custom_call_target="tpu_custom_call" | custom-call | tf_op jit(solution)/shard_map/pallas_call | solution.py:293
  2.1 1.3 %collective-permute-start.3 = (f32[2,2,128,128]{3,2,1,0:T(8,128)}, f32[2,2,128,128]{3,2,1,0:T(8,128)S(1)}, u32[]{:S(2)}, u32[]{:S(2)}) collective-permute-start(f32[2,2,128,128]{3,2,1,0:T(8,128)} %get-tuple-element.23), channel_id=1, source_target_pairs={{10,0},{12,2},{14,4},{18,8},{20,10},{22,12},{26,16},{28,18},{30,20... | collective-permute-start | bytes 786440 | tf_op jit(solution)/shard_map/ppermute | solution.py:34
  3.4 1.3 %collective-permute-start.4 = (f32[2,256,128]{2,1,0:T(8,128)S(1)}, f32[2,256,128]{2,1,0:T(8,128)S(1)}, u32[]{:S(2)}, u32[]{:S(2)}) collective-permute-start(f32[2,256,128]{2,1,0:T(8,128)S(1)} %get-tuple-element.24), channel_id=1, source_target_pairs={{2,0},{4,2},{6,4},{3,1},{5,3},{7,5},{10,8},{12,10},{14,12},{11,9},... | collective-permute-start | bytes 786440 | tf_op jit(solution)/shard_map/ppermute | solution.py:23
  4.7 1.3 %collective-permute-start.5 = (f32[2,128,256]{2,1,0:T(8,128)S(1)}, f32[2,128,256]{2,1,0:T(8,128)}, u32[]{:S(2)}, u32[]{:S(2)}) collective-permute-start(f32[2,128,256]{2,1,0:T(8,128)S(1)} %get-tuple-element.25), channel_id=1, source_target_pairs={{8,0},{16,8},{24,16},{9,1},{17,9},{25,17},{10,2},{18,10},{26,18},{... | collective-permute-start | bytes 786440 | tf_op jit(solution)/shard_map/ppermute | solution.py:23
  6.0 3.0 %collective-permute-start = (f32[1,2,128,128]{3,2,1,0:T(8,128)}, f32[1,2,128,128]{3,2,1,0:T(8,128)S(1)}, u32[]{:S(2)}, u32[]{:S(2)}) collective-permute-start(f32[1,2,128,128]{3,2,1,0:T(8,128)} %param.7), channel_id=1, source_target_pairs={{0,1},{1,0},{2,3},{3,2},{4,5},{5,4},{6,7},{7,6},{8,9},{9,8},{10,11... | collective-permute-start | bytes 393224 | tf_op jit(solution)/shard_map/ppermute | solution.py:306
  9.0 1.3 %collective-permute-start.2 = (f32[2,128,256]{2,1,0:T(8,128)S(1)}, f32[2,128,256]{2,1,0:T(8,128)S(1)}, u32[]{:S(2)}, u32[]{:S(2)}) collective-permute-start(f32[2,128,256]{2,1,0:T(8,128)S(1)} %shard_map.66), channel_id=1, source_target_pairs={{8,0},{16,8},{24,16},{9,1},{17,9},{25,17},{10,2},{18,10},{26,18},{... | collective-permute-start | bytes 786440 | tf_op jit(solution)/shard_map/ppermute | solution.py:23
  10.3 0.0 copy-done.5
  10.4 0.1 copy.12.offsets
  10.4 2.8 %collective-permute-done = f32[1,2,128,128]{3,2,1,0:T(8,128)S(1)} collective-permute-done((f32[1,2,128,128]{3,2,1,0:T(8,128)}, f32[1,2,128,128]{3,2,1,0:T(8,128)S(1)}, u32[]{:S(2)}, u32[]{:S(2)}) %collective-permute-start) | collective-permute-done | bytes 131104 | tf_op jit(solution)/shard_map/ppermute | solution.py:306
  13.2 0.0 copy-done.1
  13.2 0.0 copy-done.2
  13.2 0.0 copy-done.3
  13.2 0.5 shard_map.65
  13.7 1.3 %collective-permute-start.1 = (f32[2,256,128]{2,1,0:T(8,128)S(1)}, f32[2,256,128]{2,1,0:T(8,128)S(1)}, u32[]{:S(2)}, u32[]{:S(2)}) collective-permute-start(f32[2,256,128]{2,1,0:T(8,128)S(1)} %get-tuple-element.22), channel_id=1, source_target_pairs={{2,0},{4,2},{6,4},{3,1},{5,3},{7,5},{10,8},{12,10},{14,12},{11,9},... | collective-permute-start | bytes 786440 | tf_op jit(solution)/shard_map/ppermute | solution.py:23
  15.0 0.0 collective-permute-done.3.corner
  15.0 0.0 collective-permute-done.4.right
  15.0 1.5 %collective-permute-done.5.lower = f32[2,128,256]{2,1,0:T(8,128)} collective-permute-done((f32[2,128,256]{2,1,0:T(8,128)S(1)}, f32[2,128,256]{2,1,0:T(8,128)}, u32[]{:S(2)}, u32[]{:S(2)}) %collective-permute-start.5) | collective-permute-done | bytes 262176 | tf_op jit(solution)/shard_map/ppermute | solution.py:23
  16.6 0.0 copy-start.4
  16.6 5.2 %shard_map.67.middle = f32[8,2,2,128,128]{4,3,2,1,0:T(8,128)S(1)} custom-call(s32[8,2]{1,0:T(8,128)S(1)} %copy.12.offsets, f32[2,2,256,256]{3,2,1,0:T(8,128)S(1)} %get-tuple-element.21.refs_2_.tile.objects, f32[2,256,128]{2,1,0:T(8,128)S(1)} %collective-permute-done.4.right, f32[2,128,256]{2,1,0:T(8,128)} %collective-permute-done.5.lower, ...), custom_call_target="tpu_custom_call" | custom-call | flops 9663676416 | bytes 4194304 | tf_op jit(solution)/shard_map/pallas_call | solution.py:328
  21.7 0.3 collective-permute-done.2.lower
  22.1 0.0 collective-permute-done.1.right
  22.1 0.0 copy-done.4
  22.1 5.4 %shard_map.68 = (f32[8,2,2,128,128]{4,3,2,1,0:T(8,128)S(1)}, f32[2,256,256]{2,1,0:T(8,128)S(1)}, f32[2,256,128]{2,1,0:T(8,128)S(1)}, f32[2,128,256]{2,1,0:T(8,128)S(1)}, f32[2,128,128]{2,1,0:T(8,128)S(1)}) custom-call(s32[8,2]{1,0:T(8,128)S(1)} %copy.12.offsets, f32[2,2,256,256]{3,2,1,0:T(8,128)S(1)} %get-tuple-element.21.refs_2_.tile.objects, ...), custom_call_target="tpu_custom_call" | custom-call | flops 4831838208 | bytes 4194304 | tf_op jit(solution)/shard_map/pallas_call | solution.py:338
  27.5 3.8 %collective-permute-start.7 = (f32[2,128,256]{2,1,0:T(8,128)S(1)}, f32[2,128,256]{2,1,0:T(8,128)S(1)}, u32[]{:S(2)}, u32[]{:S(2)}) collective-permute-start(f32[2,128,256]{2,1,0:T(8,128)S(1)} %get-tuple-element.34), channel_id=1, source_target_pairs={{0,8},{8,16},{16,24},{1,9},{9,17},{17,25},{2,10},{10,18},{18,26},{... | collective-permute-start | bytes 786440 | tf_op jit(solution)/shard_map/ppermute | solution.py:23
  31.4 5.0 %shard_map.69 = (f32[2,256,256]{2,1,0:T(8,128)S(1)}, f32[2,2,256,128]{3,2,1,0:T(8,128)S(1)}, f32[2,128,256]{2,1,0:T(8,128)S(1)}, f32[2,2,128,128]{3,2,1,0:T(8,128)S(1)}) custom-call(s32[8,2]{1,0:T(8,128)S(1)} %copy.12.offsets, f32[8,2,2,128,128]{4,3,2,1,0:T(8,128)S(1)} %get-tuple-element.28.back, f32[3,2,128,128]{3,2,1,0:T(8,128)S(1)} %get-tuple-element.26.factors, ...), custom_call_target="tpu_custom_call" | custom-call | flops 4831838208 | bytes 4194304 | tf_op jit(solution)/shard_map/pallas_call | solution.py:348
  36.4 3.3 %collective-permute-start.6 = (f32[2,128,256]{2,1,0:T(8,128)S(1)}, f32[2,128,256]{2,1,0:T(8,128)S(1)}, u32[]{:S(2)}, u32[]{:S(2)}) collective-permute-start(f32[2,128,256]{2,1,0:T(8,128)S(1)} %get-tuple-element.32), channel_id=1, source_target_pairs={{0,8},{8,16},{16,24},{1,9},{9,17},{17,25},{2,10},{10,18},{18,26},{... | collective-permute-start | bytes 786440 | tf_op jit(solution)/shard_map/ppermute | solution.py:23
  39.7 3.1 %collective-permute-start.8 = (f32[2,2,256,128]{3,2,1,0:T(8,128)S(1)}, f32[2,2,256,128]{3,2,1,0:T(8,128)S(1)}, u32[]{:S(2)}, u32[]{:S(2)}) collective-permute-start(f32[2,2,256,128]{3,2,1,0:T(8,128)S(1)} %get-tuple-element.35), channel_id=1, source_target_pairs={{0,2},{2,4},{4,6},{1,3},{3,5},{5,7},{8,10},{10,12},{12,14},{9,11},... | collective-permute-start | bytes 1572872 | tf_op jit(solution)/shard_map/ppermute | solution.py:23
  42.7 5.4 %collective-permute-start.9 = (f32[2,2,128,128]{3,2,1,0:T(8,128)S(1)}, f32[2,2,128,128]{3,2,1,0:T(8,128)S(1)}, u32[]{:S(2)}, u32[]{:S(2)}) collective-permute-start(f32[2,2,128,128]{3,2,1,0:T(8,128)S(1)} %get-tuple-element.36), channel_id=1, source_target_pairs={{0,10},{2,12},{4,14},{8,18},{10,20},{12,22},{16,26},{18,28},{20,30... | collective-permute-start | bytes 786440 | tf_op jit(solution)/shard_map/ppermute | solution.py:34
  48.2 0.0 collective-permute-done.7.lower
  48.2 0.1 shard_map.71.own1
  48.3 0.0 collective-permute-done.6.lower
  48.3 0.1 shard_map.70.own0
  48.4 1.0 %shard_map.72.written = f32[2,2,256,256]{3,2,1,0:T(8,128)} custom-call(f32[2,256,256]{2,1,0:T(8,128)S(1)} %shard_map.70.own0, f32[2,256,256]{2,1,0:T(8,128)S(1)} %shard_map.71.own1), custom_call_target="tpu_custom_call" | custom-call | bytes 4194304 | tf_op jit(solution)/shard_map/pallas_call | solution.py:374
  49.4 4.6 %collective-permute-done.9.corner = f32[2,2,128,128]{3,2,1,0:T(8,128)S(1)} collective-permute-done((f32[2,2,128,128]{3,2,1,0:T(8,128)S(1)}, f32[2,2,128,128]{3,2,1,0:T(8,128)S(1)}, u32[]{:S(2)}, u32[]{:S(2)}) %collective-permute-start.9) | collective-permute-done | bytes 262176 | tf_op jit(solution)/shard_map/ppermute | solution.py:34
  54.0 0.0 collective-permute-done.8.right
  54.0 0.9 %shard_map.73 = f32[2,2,256,256]{3,2,1,0:T(8,128)} custom-call(f32[2,2,256,256]{3,2,1,0:T(8,128)} %shard_map.72.written, f32[2,256,256]{2,1,0:T(8,128)S(1)} %shard_map.70.own0, f32[2,256,256]{2,1,0:T(8,128)S(1)} %shard_map.71.own1, f32[2,2,256,128]{3,2,1,0:T(8,128)S(1)} %collective-permute-done.8.right, ...), custom_call_target="tpu_custom_call", output_to_operand_aliasing={{}: (0, {})} | custom-call | tf_op jit(solution)/shard_map/pallas_call | solution.py:382
  (1 shorter events, 0.0 us)
Async XLA Ops:
  0.0 1.2 %copy-start = (f32[2,2,256,256]{3,2,1,0:T(8,128)S(1)}, f32[2,2,256,256]{3,2,1,0:T(8,128)}, u32[]{:S(2)}) copy-start(f32[2,2,256,256]{3,2,1,0:T(8,128)} %objects.1) | copy-start | bytes 3145732
  1.2 9.1 %copy-start.5 = (s32[1,1,8,2]{2,3,1,0:T(2,128)S(1)}, s32[1,1,8,2]{2,3,1,0:T(2,128)}, u32[]{:S(2)}) copy-start(s32[1,1,8,2]{2,3,1,0:T(2,128)} %param.9) | copy-start | bytes 196
  1.2 12.0 %copy-start.1 = (bf16[2,2,256,256]{3,2,1,0:T(8,128)(2,1)S(1)}, bf16[2,2,256,256]{3,2,1,0:T(8,128)(2,1)}, u32[]{:S(2)}) copy-start(bf16[2,2,256,256]{3,2,1,0:T(8,128)(2,1)} %constant.2.clone.refs_4_) | copy-start | bytes 1572868
  1.2 12.0 %copy-start.2 = (f32[1,2,128,128]{3,2,1,0:T(8,128)S(1)}, f32[1,2,128,128]{3,2,1,0:T(8,128)}, u32[]{:S(2)}) copy-start(f32[1,2,128,128]{3,2,1,0:T(8,128)} %param.7) | copy-start | bytes 393220
  1.2 12.0 %copy-start.3 = (f32[128,128]{1,0:T(8,128)S(1)}, f32[128,128]{1,0:T(8,128)}, u32[]{:S(2)}) copy-start(f32[128,128]{1,0:T(8,128)} %refs_3_.1) | copy-start | bytes 196612
  2.1 12.9 %collective-permute-start.3 = (f32[2,2,128,128]{3,2,1,0:T(8,128)}, f32[2,2,128,128]{3,2,1,0:T(8,128)S(1)}, u32[]{:S(2)}, u32[]{:S(2)}) collective-permute-start(f32[2,2,128,128]{3,2,1,0:T(8,128)} %get-tuple-element.23), channel_id=1, source_target_pairs={{10,0},{12,2},{14,4},{18,8},{20,10},{22,12},{26,16},{28,18},{30,20... | collective-permute-start | bytes 786440 | tf_op jit(solution)/shard_map/ppermute | solution.py:34
  3.4 11.6 %collective-permute-start.4 = (f32[2,256,128]{2,1,0:T(8,128)S(1)}, f32[2,256,128]{2,1,0:T(8,128)S(1)}, u32[]{:S(2)}, u32[]{:S(2)}) collective-permute-start(f32[2,256,128]{2,1,0:T(8,128)S(1)} %get-tuple-element.24), channel_id=1, source_target_pairs={{2,0},{4,2},{6,4},{3,1},{5,3},{7,5},{10,8},{12,10},{14,12},{11,9},... | collective-permute-start | bytes 786440 | tf_op jit(solution)/shard_map/ppermute | solution.py:23
  4.7 11.8 %collective-permute-start.5 = (f32[2,128,256]{2,1,0:T(8,128)S(1)}, f32[2,128,256]{2,1,0:T(8,128)}, u32[]{:S(2)}, u32[]{:S(2)}) collective-permute-start(f32[2,128,256]{2,1,0:T(8,128)S(1)} %get-tuple-element.25), channel_id=1, source_target_pairs={{8,0},{16,8},{24,16},{9,1},{17,9},{25,17},{10,2},{18,10},{26,18},{... | collective-permute-start | bytes 786440 | tf_op jit(solution)/shard_map/ppermute | solution.py:23
  6.0 7.2 %collective-permute-start = (f32[1,2,128,128]{3,2,1,0:T(8,128)}, f32[1,2,128,128]{3,2,1,0:T(8,128)S(1)}, u32[]{:S(2)}, u32[]{:S(2)}) collective-permute-start(f32[1,2,128,128]{3,2,1,0:T(8,128)} %param.7), channel_id=1, source_target_pairs={{0,1},{1,0},{2,3},{3,2},{4,5},{5,4},{6,7},{7,6},{8,9},{9,8},{10,11... | collective-permute-start | bytes 393224 | tf_op jit(solution)/shard_map/ppermute | solution.py:306
  9.0 13.0 %collective-permute-start.2 = (f32[2,128,256]{2,1,0:T(8,128)S(1)}, f32[2,128,256]{2,1,0:T(8,128)S(1)}, u32[]{:S(2)}, u32[]{:S(2)}) collective-permute-start(f32[2,128,256]{2,1,0:T(8,128)S(1)} %shard_map.66), channel_id=1, source_target_pairs={{8,0},{16,8},{24,16},{9,1},{17,9},{25,17},{10,2},{18,10},{26,18},{... | collective-permute-start | bytes 786440 | tf_op jit(solution)/shard_map/ppermute | solution.py:23
  13.7 8.4 %collective-permute-start.1 = (f32[2,256,128]{2,1,0:T(8,128)S(1)}, f32[2,256,128]{2,1,0:T(8,128)S(1)}, u32[]{:S(2)}, u32[]{:S(2)}) collective-permute-start(f32[2,256,128]{2,1,0:T(8,128)S(1)} %get-tuple-element.22), channel_id=1, source_target_pairs={{2,0},{4,2},{6,4},{3,1},{5,3},{7,5},{10,8},{12,10},{14,12},{11,9},... | collective-permute-start | bytes 786440 | tf_op jit(solution)/shard_map/ppermute | solution.py:23
  16.6 5.5 %copy-start.4 = (f32[1,1,8,128,128]{4,3,2,1,0:T(8,128)S(1)}, f32[1,1,8,128,128]{4,3,2,1,0:T(8,128)}, u32[]{:S(2)}) copy-start(f32[1,1,8,128,128]{4,3,2,1,0:T(8,128)} %param.10) | copy-start | bytes 1572868
  27.5 20.7 %collective-permute-start.7 = (f32[2,128,256]{2,1,0:T(8,128)S(1)}, f32[2,128,256]{2,1,0:T(8,128)S(1)}, u32[]{:S(2)}, u32[]{:S(2)}) collective-permute-start(f32[2,128,256]{2,1,0:T(8,128)S(1)} %get-tuple-element.34), channel_id=1, source_target_pairs={{0,8},{8,16},{16,24},{1,9},{9,17},{17,25},{2,10},{10,18},{18,26},{... | collective-permute-start | bytes 786440 | tf_op jit(solution)/shard_map/ppermute | solution.py:23
  36.4 11.9 %collective-permute-start.6 = (f32[2,128,256]{2,1,0:T(8,128)S(1)}, f32[2,128,256]{2,1,0:T(8,128)S(1)}, u32[]{:S(2)}, u32[]{:S(2)}) collective-permute-start(f32[2,128,256]{2,1,0:T(8,128)S(1)} %get-tuple-element.32), channel_id=1, source_target_pairs={{0,8},{8,16},{16,24},{1,9},{9,17},{17,25},{2,10},{10,18},{18,26},{... | collective-permute-start | bytes 786440 | tf_op jit(solution)/shard_map/ppermute | solution.py:23
  39.7 14.3 %collective-permute-start.8 = (f32[2,2,256,128]{3,2,1,0:T(8,128)S(1)}, f32[2,2,256,128]{3,2,1,0:T(8,128)S(1)}, u32[]{:S(2)}, u32[]{:S(2)}) collective-permute-start(f32[2,2,256,128]{3,2,1,0:T(8,128)S(1)} %get-tuple-element.35), channel_id=1, source_target_pairs={{0,2},{2,4},{4,6},{1,3},{3,5},{5,7},{8,10},{10,12},{12,14},{9,11},... | collective-permute-start | bytes 1572872 | tf_op jit(solution)/shard_map/ppermute | solution.py:23
  42.7 11.2 %collective-permute-start.9 = (f32[2,2,128,128]{3,2,1,0:T(8,128)S(1)}, f32[2,2,128,128]{3,2,1,0:T(8,128)S(1)}, u32[]{:S(2)}, u32[]{:S(2)}) collective-permute-start(f32[2,2,128,128]{3,2,1,0:T(8,128)S(1)} %get-tuple-element.36), channel_id=1, source_target_pairs={{0,10},{2,12},{4,14},{8,18},{10,20},{12,22},{16,26},{18,28},{20,30... | collective-permute-start | bytes 786440 | tf_op jit(solution)/shard_map/ppermute | solution.py:34

commit v3 on v1

--- a/solution.py
+++ b/solution.py
@@ -160,19 +160,12 @@
     corner[...] = total[:, t:, t:]
 
 
-def pack_kernel(objects, tile, lower0, corner, right0, sems):
+def pack_kernel(objects, tile, lower0, corner, right0):
     n = corner.shape[-1]
-    pieces = (
-        (objects.at[:, :, pl.ds(0, n), pl.ds(0, n)], corner),
-        (objects.at[0, :, pl.ds(0, n), :], lower0),
-        (objects.at[0, :, :, pl.ds(0, n)], right0),
-        (objects, tile),
-    )
-    copies = [pltpu.make_async_copy(piece, out, sems.at[i]) for i, (piece, out) in enumerate(pieces)]
-    for copy in copies:
-        copy.start()
-    for copy in copies:
-        copy.wait()
+    lower0[...] = objects[0, :, :n, :]
+    corner[...] = objects[:, :, :n, :n]
+    right0[...] = objects[0, :, :, :n]
+    tile[...] = objects[...]
 
 
 def stage_kernel(tile, lower1):
@@ -256,17 +249,13 @@
     out[:, :n] = own[:, :n] + lower[...]
 
 
-def add_right_kernel(own0, own1, right, out):
-    n = right.shape[-1]
-    for s, own in enumerate((own0, own1)):
-        out[s, :, :, n:] = own[:, :, n:]
-        out[s, :, :, :n] = own[:, :, :n] + right[s]
-
-
-def add_corner_kernel(own, corner, out):
+def combine_kernel(own0, own1, right, corner, out):
     n = corner.shape[-1]
-    out[...] = own[...]
-    out[:, :, :n, :n] += corner[...]
+    out[0] = own0[...]
+    out[1] = own1[...]
+    for s in range(out.shape[0]):
+        out[s, :, :, :n] += right[s]
+        out[s, :, :n, :n] += corner[s]
 
 
 def cost(transforms, n):
@@ -288,9 +277,8 @@
     tile, lower0, corner, right0 = pl.pallas_call(
         pack_kernel,
         out_shape=(shape(*objects.shape), rim_lower, rim_corner, shape(2, t, n)),
-        in_specs=[pl.BlockSpec(memory_space=pltpu.HBM)],
+        in_specs=[VMEM],
         out_specs=(VMEM,) * 4,
-        scratch_shapes=[pltpu.SemaphoreType.DMA((4,))],
         compiler_params=small,
     )(objects)
     lower0 = passed_along(lower0, "row", -1)
@@ -363,23 +351,15 @@
             cost_estimate=cost(weight, n),
         )(own, lower)
 
-    own1 = with_lower(own1, grad_lower1, 20)
-    own0 = with_lower(own0, grad_lower0, 90)
-    own = pl.pallas_call(
-        add_right_kernel,
-        out_shape=shape(*objects.shape),
-        in_specs=[VMEM] * 3,
+    own1 = with_lower(own1, grad_lower1, 64)
+    own0 = with_lower(own0, grad_lower0, 0)
+    return pl.pallas_call(
+        combine_kernel,
+        out_shape=jax.ShapeDtypeStruct(objects.shape, F32),
+        in_specs=[VMEM] * 4,
         out_specs=VMEM,
         compiler_params=small,
-        cost_estimate=cost(0, n),
-    )(own0, own1, grad_right)
-    return pl.pallas_call(
-        add_corner_kernel,
-        out_shape=shape(*objects.shape),
-        in_specs=[VMEM] * 2,
-        out_specs=VMEM,
-        compiler_params=small,
-    )(own, grad_corner)
+    )(own0, own1, grad_right, grad_corner)
 
 
 def solution(mesh):

time: 55.5 us -> 55.5 us (level)
    pallas_call x2 -> x1, Pallas kernels: 1.16 us -> 1.1 us  [on_device(): pl.pallas_call(combine_kernel, out_shape=jax.ShapeDtypeStruct(objects.sha...]
  transfers between devices with their start and end apart: 10 -> 10, of which waited for: 4 -> 4; matrix products, arithmetic and copies ran while one was open for 0% -> 0% of each run, Pallas kernels for 20% -> 11%
where the time goes in v3:
time: 55.5 us; the launch traced here: 55.1 us
  starting transfers between devices  25 us (45%)
  Pallas kernels  18.1 us (33%)
  waiting for transfers between devices  10.5 us (19%)
  local copies, waits for them, and re-layouts  1.32 us (2%)
    ppermute x7, starting transfers between devices, passed_along(): return lax.ppermute(value, axis, pairs)  15.3 us
    ppermute x2, starting transfers between devices, passed_across(): return lax.ppermute(value, ('row', 'col'), pairs)  6.74 us
    ppermute x2, waiting for transfers between devices, passed_across(): return lax.ppermute(value, ('row', 'col'), pairs)  5.84 us
    pallas_call x1, Pallas kernels, on_device(): pl.pallas_call(second_kernel, out_shape=(waves, shape(2, t, t), shape(2,...  5.36 us
    pallas_call x1, Pallas kernels, on_device(): pl.pallas_call(middle_kernel, out_shape=waves, in_specs=[SMEM] + [VMEM] *...  5.17 us
    pallas_call x1, Pallas kernels, on_device(): pl.pallas_call(first_kernel, out_shape=(shape(2, t, t), rim_right, rim_lo...  5.01 us
    ppermute x1, starting transfers between devices, on_device(): lax.ppermute(probes, 'mode', [(i, (i + by) % mode_count) for i in range(m...  3 us
    ppermute x1, waiting for transfers between devices, on_device(): lax.ppermute(probes, 'mode', [(i, (i + by) % mode_count) for i in range(m...  2.79 us
  transfers between devices with their start and end apart: 10, of which 4 were waited for; matrix products, arithmetic and copies ran while one was open for 0% of the time, Pallas kernels for 11%

profile of v3, /device:TPU:0, one launch (start us, length us, event | category | flops | bytes accessed | tf_op | source)
XLA Modules:
  0.0 55.1 jit_solution(13701844503040962920)
XLA Ops:
  0.0 0.0 copy-start
  0.0 1.2 %copy-done = f32[2,2,256,256]{3,2,1,0:T(8,128)S(1)} copy-done((f32[2,2,256,256]{3,2,1,0:T(8,128)S(1)}, f32[2,2,256,256]{3,2,1,0:T(8,128)}, u32[]{:S(2)}) %copy-start) | copy-done | bytes 1048600
  1.2 0.0 copy-start.5
  1.2 0.0 copy-start.1
  1.2 0.0 copy-start.2
  1.2 0.0 copy-start.3
  1.2 0.8 %shard_map.64 = (f32[2,2,256,256]{3,2,1,0:T(8,128)S(1)}, f32[2,128,256]{2,1,0:T(8,128)S(1)}, f32[2,2,128,128]{3,2,1,0:T(8,128)}, f32[2,256,128]{2,1,0:T(8,128)S(1)}) custom-call(f32[2,2,256,256]{3,2,1,0:T(8,128)S(1)} %copy-done), custom_call_target="tpu_custom_call" | custom-call | tf_op jit(solution)/shard_map/pallas_call | solution.py:277
  2.1 1.3 %collective-permute-start.3 = (f32[2,2,128,128]{3,2,1,0:T(8,128)}, f32[2,2,128,128]{3,2,1,0:T(8,128)S(1)}, u32[]{:S(2)}, u32[]{:S(2)}) collective-permute-start(f32[2,2,128,128]{3,2,1,0:T(8,128)} %get-tuple-element.23), channel_id=1, source_target_pairs={{10,0},{12,2},{14,4},{18,8},{20,10},{22,12},{26,16},{28,18},{30,20... | collective-permute-start | bytes 786440 | tf_op jit(solution)/shard_map/ppermute | solution.py:34
  3.3 1.3 %collective-permute-start.4 = (f32[2,256,128]{2,1,0:T(8,128)S(1)}, f32[2,256,128]{2,1,0:T(8,128)S(1)}, u32[]{:S(2)}, u32[]{:S(2)}) collective-permute-start(f32[2,256,128]{2,1,0:T(8,128)S(1)} %get-tuple-element.24), channel_id=1, source_target_pairs={{2,0},{4,2},{6,4},{3,1},{5,3},{7,5},{10,8},{12,10},{14,12},{11,9},... | collective-permute-start | bytes 786440 | tf_op jit(solution)/shard_map/ppermute | solution.py:23
  4.6 1.3 %collective-permute-start.5 = (f32[2,128,256]{2,1,0:T(8,128)S(1)}, f32[2,128,256]{2,1,0:T(8,128)}, u32[]{:S(2)}, u32[]{:S(2)}) collective-permute-start(f32[2,128,256]{2,1,0:T(8,128)S(1)} %get-tuple-element.25), channel_id=1, source_target_pairs={{8,0},{16,8},{24,16},{9,1},{17,9},{25,17},{10,2},{18,10},{26,18},{... | collective-permute-start | bytes 786440 | tf_op jit(solution)/shard_map/ppermute | solution.py:23
  5.9 3.0 %collective-permute-start = (f32[1,2,128,128]{3,2,1,0:T(8,128)}, f32[1,2,128,128]{3,2,1,0:T(8,128)S(1)}, u32[]{:S(2)}, u32[]{:S(2)}) collective-permute-start(f32[1,2,128,128]{3,2,1,0:T(8,128)} %param.7), channel_id=1, source_target_pairs={{0,1},{1,0},{2,3},{3,2},{4,5},{5,4},{6,7},{7,6},{8,9},{9,8},{10,11... | collective-permute-start | bytes 393224 | tf_op jit(solution)/shard_map/ppermute | solution.py:289
  9.0 1.3 %collective-permute-start.2 = (f32[2,128,256]{2,1,0:T(8,128)S(1)}, f32[2,128,256]{2,1,0:T(8,128)S(1)}, u32[]{:S(2)}, u32[]{:S(2)}) collective-permute-start(f32[2,128,256]{2,1,0:T(8,128)S(1)} %shard_map.66), channel_id=1, source_target_pairs={{8,0},{16,8},{24,16},{9,1},{17,9},{25,17},{10,2},{18,10},{26,18},{... | collective-permute-start | bytes 786440 | tf_op jit(solution)/shard_map/ppermute | solution.py:23
  10.3 0.0 copy-done.5
  10.3 0.1 copy.11.offsets
  10.4 2.8 %collective-permute-done = f32[1,2,128,128]{3,2,1,0:T(8,128)S(1)} collective-permute-done((f32[1,2,128,128]{3,2,1,0:T(8,128)}, f32[1,2,128,128]{3,2,1,0:T(8,128)S(1)}, u32[]{:S(2)}, u32[]{:S(2)}) %collective-permute-start) | collective-permute-done | bytes 131104 | tf_op jit(solution)/shard_map/ppermute | solution.py:289
  13.2 0.0 copy-done.1
  13.2 0.0 copy-done.2
  13.2 0.0 copy-done.3
  13.2 0.5 shard_map.65
  13.6 1.3 %collective-permute-start.1 = (f32[2,256,128]{2,1,0:T(8,128)S(1)}, f32[2,256,128]{2,1,0:T(8,128)S(1)}, u32[]{:S(2)}, u32[]{:S(2)}) collective-permute-start(f32[2,256,128]{2,1,0:T(8,128)S(1)} %get-tuple-element.22), channel_id=1, source_target_pairs={{2,0},{4,2},{6,4},{3,1},{5,3},{7,5},{10,8},{12,10},{14,12},{11,9},... | collective-permute-start | bytes 786440 | tf_op jit(solution)/shard_map/ppermute | solution.py:23
  14.9 0.0 collective-permute-done.3.corner
  14.9 0.0 collective-permute-done.4.right
  15.0 1.5 %collective-permute-done.5.lower = f32[2,128,256]{2,1,0:T(8,128)} collective-permute-done((f32[2,128,256]{2,1,0:T(8,128)S(1)}, f32[2,128,256]{2,1,0:T(8,128)}, u32[]{:S(2)}, u32[]{:S(2)}) %collective-permute-start.5) | collective-permute-done | bytes 262176 | tf_op jit(solution)/shard_map/ppermute | solution.py:23
  16.5 0.0 copy-start.4
  16.5 5.2 %shard_map.67.middle = f32[8,2,2,128,128]{4,3,2,1,0:T(8,128)S(1)} custom-call(s32[8,2]{1,0:T(8,128)S(1)} %copy.11.offsets, f32[2,2,256,256]{3,2,1,0:T(8,128)S(1)} %get-tuple-element.21.refs_2_.tile.objects, f32[2,256,128]{2,1,0:T(8,128)S(1)} %collective-permute-done.4.right, f32[2,128,256]{2,1,0:T(8,128)} %collective-permute-done.5.lower, ...), custom_call_target="tpu_custom_call" | custom-call | flops 9663676416 | bytes 4194304 | tf_op jit(solution)/shard_map/pallas_call | solution.py:310
  21.7 0.3 collective-permute-done.2.lower
  22.0 0.0 collective-permute-done.1.right
  22.0 0.0 copy-done.4
  22.0 5.4 %shard_map.68 = (f32[8,2,2,128,128]{4,3,2,1,0:T(8,128)S(1)}, f32[2,256,256]{2,1,0:T(8,128)S(1)}, f32[2,256,128]{2,1,0:T(8,128)S(1)}, f32[2,128,256]{2,1,0:T(8,128)S(1)}, f32[2,128,128]{2,1,0:T(8,128)S(1)}) custom-call(s32[8,2]{1,0:T(8,128)S(1)} %copy.11.offsets, f32[2,2,256,256]{3,2,1,0:T(8,128)S(1)} %get-tuple-element.21.refs_2_.tile.objects, ...), custom_call_target="tpu_custom_call" | custom-call | flops 4831838208 | bytes 4194304 | tf_op jit(solution)/shard_map/pallas_call | solution.py:320
  27.4 5.0 %shard_map.69 = (f32[2,256,256]{2,1,0:T(8,128)S(1)}, f32[2,2,256,128]{3,2,1,0:T(8,128)S(1)}, f32[2,128,256]{2,1,0:T(8,128)S(1)}, f32[2,2,128,128]{3,2,1,0:T(8,128)S(1)}) custom-call(s32[8,2]{1,0:T(8,128)S(1)} %copy.11.offsets, f32[8,2,2,128,128]{4,3,2,1,0:T(8,128)S(1)} %get-tuple-element.28.back, f32[3,2,128,128]{3,2,1,0:T(8,128)S(1)} %get-tuple-element.26.factors, ...), custom_call_target="tpu_custom_call" | custom-call | flops 4831838208 | bytes 4194304 | tf_op jit(solution)/shard_map/pallas_call | solution.py:330
  32.4 3.7 %collective-permute-start.6 = (f32[2,128,256]{2,1,0:T(8,128)S(1)}, f32[2,128,256]{2,1,0:T(8,128)S(1)}, u32[]{:S(2)}, u32[]{:S(2)}) collective-permute-start(f32[2,128,256]{2,1,0:T(8,128)S(1)} %get-tuple-element.32), channel_id=1, source_target_pairs={{0,8},{8,16},{16,24},{1,9},{9,17},{17,25},{2,10},{10,18},{18,26},{... | collective-permute-start | bytes 786440 | tf_op jit(solution)/shard_map/ppermute | solution.py:23
  36.1 3.3 %collective-permute-start.7 = (f32[2,128,256]{2,1,0:T(8,128)S(1)}, f32[2,128,256]{2,1,0:T(8,128)S(1)}, u32[]{:S(2)}, u32[]{:S(2)}) collective-permute-start(f32[2,128,256]{2,1,0:T(8,128)S(1)} %get-tuple-element.34), channel_id=1, source_target_pairs={{0,8},{8,16},{16,24},{1,9},{9,17},{17,25},{2,10},{10,18},{18,26},{... | collective-permute-start | bytes 786440 | tf_op jit(solution)/shard_map/ppermute | solution.py:23
  39.4 3.1 %collective-permute-start.8 = (f32[2,2,256,128]{3,2,1,0:T(8,128)S(1)}, f32[2,2,256,128]{3,2,1,0:T(8,128)S(1)}, u32[]{:S(2)}, u32[]{:S(2)}) collective-permute-start(f32[2,2,256,128]{3,2,1,0:T(8,128)S(1)} %get-tuple-element.35), channel_id=1, source_target_pairs={{0,2},{2,4},{4,6},{1,3},{3,5},{5,7},{8,10},{10,12},{12,14},{9,11},... | collective-permute-start | bytes 1572872 | tf_op jit(solution)/shard_map/ppermute | solution.py:23
  42.5 5.5 %collective-permute-start.9 = (f32[2,2,128,128]{3,2,1,0:T(8,128)S(1)}, f32[2,2,128,128]{3,2,1,0:T(8,128)S(1)}, u32[]{:S(2)}, u32[]{:S(2)}) collective-permute-start(f32[2,2,128,128]{3,2,1,0:T(8,128)S(1)} %get-tuple-element.36), channel_id=1, source_target_pairs={{0,10},{2,12},{4,14},{8,18},{10,20},{12,22},{16,26},{18,28},{20,30... | collective-permute-start | bytes 786440 | tf_op jit(solution)/shard_map/ppermute | solution.py:34
  48.0 0.0 collective-permute-done.6.lower
  48.0 0.1 shard_map.70.own0
  48.1 0.0 collective-permute-done.7.lower
  48.1 0.1 shard_map.71.own1
  48.2 5.8 %collective-permute-done.9.corner = f32[2,2,128,128]{3,2,1,0:T(8,128)S(1)} collective-permute-done((f32[2,2,128,128]{3,2,1,0:T(8,128)S(1)}, f32[2,2,128,128]{3,2,1,0:T(8,128)S(1)}, u32[]{:S(2)}, u32[]{:S(2)}) %collective-permute-start.9) | collective-permute-done | bytes 262176 | tf_op jit(solution)/shard_map/ppermute | solution.py:34
  54.0 0.0 collective-permute-done.8.right
  54.0 1.1 %shard_map.72 = f32[2,2,256,256]{3,2,1,0:T(8,128)} custom-call(f32[2,256,256]{2,1,0:T(8,128)S(1)} %shard_map.70.own0, f32[2,256,256]{2,1,0:T(8,128)S(1)} %shard_map.71.own1, f32[2,2,256,128]{3,2,1,0:T(8,128)S(1)} %collective-permute-done.8.right, f32[2,2,128,128]{3,2,1,0:T(8,128)S(1)} %collective-permute-done.9.corner), custom_call_target="tpu_custom_call" | custom-call | tf_op jit(solution)/shard_map/pallas_call | solution.py:356
  (1 shorter events, 0.0 us)
Async XLA Ops:
  0.0 1.2 %copy-start = (f32[2,2,256,256]{3,2,1,0:T(8,128)S(1)}, f32[2,2,256,256]{3,2,1,0:T(8,128)}, u32[]{:S(2)}) copy-start(f32[2,2,256,256]{3,2,1,0:T(8,128)} %objects.1) | copy-start | bytes 3145732
  1.2 9.1 %copy-start.5 = (s32[1,1,8,2]{2,3,1,0:T(2,128)S(1)}, s32[1,1,8,2]{2,3,1,0:T(2,128)}, u32[]{:S(2)}) copy-start(s32[1,1,8,2]{2,3,1,0:T(2,128)} %param.9) | copy-start | bytes 196
  1.2 11.9 %copy-start.1 = (bf16[2,2,256,256]{3,2,1,0:T(8,128)(2,1)S(1)}, bf16[2,2,256,256]{3,2,1,0:T(8,128)(2,1)}, u32[]{:S(2)}) copy-start(bf16[2,2,256,256]{3,2,1,0:T(8,128)(2,1)} %constant.2.clone.refs_4_) | copy-start | bytes 1572868
  1.2 11.9 %copy-start.2 = (f32[1,2,128,128]{3,2,1,0:T(8,128)S(1)}, f32[1,2,128,128]{3,2,1,0:T(8,128)}, u32[]{:S(2)}) copy-start(f32[1,2,128,128]{3,2,1,0:T(8,128)} %param.7) | copy-start | bytes 393220
  1.2 11.9 %copy-start.3 = (f32[128,128]{1,0:T(8,128)S(1)}, f32[128,128]{1,0:T(8,128)}, u32[]{:S(2)}) copy-start(f32[128,128]{1,0:T(8,128)} %refs_3_.1) | copy-start | bytes 196612
  2.1 12.9 %collective-permute-start.3 = (f32[2,2,128,128]{3,2,1,0:T(8,128)}, f32[2,2,128,128]{3,2,1,0:T(8,128)S(1)}, u32[]{:S(2)}, u32[]{:S(2)}) collective-permute-start(f32[2,2,128,128]{3,2,1,0:T(8,128)} %get-tuple-element.23), channel_id=1, source_target_pairs={{10,0},{12,2},{14,4},{18,8},{20,10},{22,12},{26,16},{28,18},{30,20... | collective-permute-start | bytes 786440 | tf_op jit(solution)/shard_map/ppermute | solution.py:34
  3.3 11.6 %collective-permute-start.4 = (f32[2,256,128]{2,1,0:T(8,128)S(1)}, f32[2,256,128]{2,1,0:T(8,128)S(1)}, u32[]{:S(2)}, u32[]{:S(2)}) collective-permute-start(f32[2,256,128]{2,1,0:T(8,128)S(1)} %get-tuple-element.24), channel_id=1, source_target_pairs={{2,0},{4,2},{6,4},{3,1},{5,3},{7,5},{10,8},{12,10},{14,12},{11,9},... | collective-permute-start | bytes 786440 | tf_op jit(solution)/shard_map/ppermute | solution.py:23
  4.6 11.8 %collective-permute-start.5 = (f32[2,128,256]{2,1,0:T(8,128)S(1)}, f32[2,128,256]{2,1,0:T(8,128)}, u32[]{:S(2)}, u32[]{:S(2)}) collective-permute-start(f32[2,128,256]{2,1,0:T(8,128)S(1)} %get-tuple-element.25), channel_id=1, source_target_pairs={{8,0},{16,8},{24,16},{9,1},{17,9},{25,17},{10,2},{18,10},{26,18},{... | collective-permute-start | bytes 786440 | tf_op jit(solution)/shard_map/ppermute | solution.py:23
  5.9 7.2 %collective-permute-start = (f32[1,2,128,128]{3,2,1,0:T(8,128)}, f32[1,2,128,128]{3,2,1,0:T(8,128)S(1)}, u32[]{:S(2)}, u32[]{:S(2)}) collective-permute-start(f32[1,2,128,128]{3,2,1,0:T(8,128)} %param.7), channel_id=1, source_target_pairs={{0,1},{1,0},{2,3},{3,2},{4,5},{5,4},{6,7},{7,6},{8,9},{9,8},{10,11... | collective-permute-start | bytes 393224 | tf_op jit(solution)/shard_map/ppermute | solution.py:289
  9.0 13.0 %collective-permute-start.2 = (f32[2,128,256]{2,1,0:T(8,128)S(1)}, f32[2,128,256]{2,1,0:T(8,128)S(1)}, u32[]{:S(2)}, u32[]{:S(2)}) collective-permute-start(f32[2,128,256]{2,1,0:T(8,128)S(1)} %shard_map.66), channel_id=1, source_target_pairs={{8,0},{16,8},{24,16},{9,1},{17,9},{25,17},{10,2},{18,10},{26,18},{... | collective-permute-start | bytes 786440 | tf_op jit(solution)/shard_map/ppermute | solution.py:23
  13.6 8.4 %collective-permute-start.1 = (f32[2,256,128]{2,1,0:T(8,128)S(1)}, f32[2,256,128]{2,1,0:T(8,128)S(1)}, u32[]{:S(2)}, u32[]{:S(2)}) collective-permute-start(f32[2,256,128]{2,1,0:T(8,128)S(1)} %get-tuple-element.22), channel_id=1, source_target_pairs={{2,0},{4,2},{6,4},{3,1},{5,3},{7,5},{10,8},{12,10},{14,12},{11,9},... | collective-permute-start | bytes 786440 | tf_op jit(solution)/shard_map/ppermute | solution.py:23
  16.5 5.5 %copy-start.4 = (f32[1,1,8,128,128]{4,3,2,1,0:T(8,128)S(1)}, f32[1,1,8,128,128]{4,3,2,1,0:T(8,128)}, u32[]{:S(2)}) copy-start(f32[1,1,8,128,128]{4,3,2,1,0:T(8,128)} %param.10) | copy-start | bytes 1572868
  32.4 15.6 %collective-permute-start.6 = (f32[2,128,256]{2,1,0:T(8,128)S(1)}, f32[2,128,256]{2,1,0:T(8,128)S(1)}, u32[]{:S(2)}, u32[]{:S(2)}) collective-permute-start(f32[2,128,256]{2,1,0:T(8,128)S(1)} %get-tuple-element.32), channel_id=1, source_target_pairs={{0,8},{8,16},{16,24},{1,9},{9,17},{17,25},{2,10},{10,18},{18,26},{... | collective-permute-start | bytes 786440 | tf_op jit(solution)/shard_map/ppermute | solution.py:23
  36.1 12.0 %collective-permute-start.7 = (f32[2,128,256]{2,1,0:T(8,128)S(1)}, f32[2,128,256]{2,1,0:T(8,128)S(1)}, u32[]{:S(2)}, u32[]{:S(2)}) collective-permute-start(f32[2,128,256]{2,1,0:T(8,128)S(1)} %get-tuple-element.34), channel_id=1, source_target_pairs={{0,8},{8,16},{16,24},{1,9},{9,17},{17,25},{2,10},{10,18},{18,26},{... | collective-permute-start | bytes 786440 | tf_op jit(solution)/shard_map/ppermute | solution.py:23
  39.4 14.6 %collective-permute-start.8 = (f32[2,2,256,128]{3,2,1,0:T(8,128)S(1)}, f32[2,2,256,128]{3,2,1,0:T(8,128)S(1)}, u32[]{:S(2)}, u32[]{:S(2)}) collective-permute-start(f32[2,2,256,128]{3,2,1,0:T(8,128)S(1)} %get-tuple-element.35), channel_id=1, source_target_pairs={{0,2},{2,4},{4,6},{1,3},{3,5},{5,7},{8,10},{10,12},{12,14},{9,11},... | collective-permute-start | bytes 1572872 | tf_op jit(solution)/shard_map/ppermute | solution.py:23
  42.5 11.5 %collective-permute-start.9 = (f32[2,2,128,128]{3,2,1,0:T(8,128)S(1)}, f32[2,2,128,128]{3,2,1,0:T(8,128)S(1)}, u32[]{:S(2)}, u32[]{:S(2)}) collective-permute-start(f32[2,2,128,128]{3,2,1,0:T(8,128)S(1)} %get-tuple-element.36), channel_id=1, source_target_pairs={{0,10},{2,12},{4,14},{8,18},{10,20},{12,22},{16,26},{18,28},{20,30... | collective-permute-start | bytes 786440 | tf_op jit(solution)/shard_map/ppermute | solution.py:34

commit v4 on v1

--- a/solution.py
+++ b/solution.py
@@ -21,6 +21,11 @@
     count = lax.axis_size(axis)
     pairs = [(i, i + by) for i in range(count) if 0 <= i + by < count]
     return lax.ppermute(value, axis, pairs)
+
+
+def passed_round(value, by):
+    count = lax.axis_size("mode")
+    return lax.ppermute(value, "mode", [(i, (i + by) % count) for i in range(count)])
 
 
 def passed_across(value, by):
@@ -144,12 +149,22 @@
     return [range(k, min(k + GROUP, count)) for k in range(0, count, GROUP)]
 
 
-def join(extended, tile, right, lower, corner):
+def share_of(rows):
+    return pl.ds(pl.multiple_of(lax.axis_index("mode") * rows, 8), rows)
+
+
+def join(extended, s, tile, right, lower, corner):
     t = tile.shape[-1]
-    extended[:, :t, :t] = tile[...]
+    extended[:, :t, :t] = tile[s]
     extended[:, :t, t:] = right[...]
     extended[:, t:, :t] = lower[...]
-    extended[:, t:, t:] = corner[...]
+    me, count, rows = lax.axis_index("mode"), len(corner), corner[0].shape[-2]
+    for slot in range(count):
+        steps = lax.rem(me - slot + count, count)
+        value = corner[0][s]
+        for by in range(1, count):
+            value = jnp.where(steps == by, corner[by][s], value)
+        extended[:, t + slot * rows : t + (slot + 1) * rows, t:] = value
 
 
 def part_ways(total, own, right, lower, corner):
@@ -160,19 +175,12 @@
     corner[...] = total[:, t:, t:]
 
 
-def pack_kernel(objects, tile, lower0, corner, right0, sems):
-    n = corner.shape[-1]
-    pieces = (
-        (objects.at[:, :, pl.ds(0, n), pl.ds(0, n)], corner),
-        (objects.at[0, :, pl.ds(0, n), :], lower0),
-        (objects.at[0, :, :, pl.ds(0, n)], right0),
-        (objects, tile),
-    )
-    copies = [pltpu.make_async_copy(piece, out, sems.at[i]) for i, (piece, out) in enumerate(pieces)]
-    for copy in copies:
-        copy.start()
-    for copy in copies:
-        copy.wait()
+def pack_kernel(objects, tile, lower0, corner, right0):
+    n = right0.shape[-1]
+    corner[...] = objects[:, :, share_of(corner.shape[-2]), :n]
+    lower0[...] = objects[0, :, :n, :]
+    right0[...] = objects[0, :, :, :n]
+    tile[...] = objects[...]
 
 
 def stage_kernel(tile, lower1):
@@ -195,9 +203,10 @@
     return pairs[:-1], pairs[-1]
 
 
-def middle_kernel(offsets, objects, right, lower, corner, factors, table, middle, extended):
-    n = corner.shape[-1]
-    join(extended, objects.at[0], right, lower, corner.at[0])
+def middle_kernel(offsets, objects, right, lower, factors, table, *refs):
+    corner, (middle, extended) = refs[:-2], refs[-2:]
+    n = right.shape[-1]
+    join(extended, 0, objects, right, lower, corner)
     probes, spread = factors_of(factors)
     for group in groups_of(offsets.shape[0]):
         windows = [cut_pair(extended, place_of(offsets, k, n), n) for k in group]
@@ -209,12 +218,10 @@
             keep(middle, k, wave)
 
 
-def second_kernel(
-    offsets, objects, right, lower, corner, middle, measured, table,
-    back, own, rim_right, rim_lower, rim_corner, extended, total,
-):
-    n = corner.shape[-1]
-    join(extended, objects.at[1], right, lower, corner.at[1])
+def second_kernel(offsets, objects, right, lower, middle, measured, table, *refs):
+    corner, (back, own, rim_right, rim_lower, rim_corner, extended, total) = refs[:-7], refs[-7:]
+    n = right.shape[-1]
+    join(extended, 1, objects, right, lower, corner)
     total[...] = jnp.zeros_like(total)
     for group in groups_of(offsets.shape[0]):
         windows = [cut_pair(extended, place_of(offsets, k, n), n) for k in group]
@@ -287,19 +294,16 @@
 
     tile, lower0, corner, right0 = pl.pallas_call(
         pack_kernel,
-        out_shape=(shape(*objects.shape), rim_lower, rim_corner, shape(2, t, n)),
-        in_specs=[pl.BlockSpec(memory_space=pltpu.HBM)],
+        out_shape=(shape(*objects.shape), rim_lower, shape(slices, 2, n // mode_count, n), shape(2, t, n)),
+        in_specs=[VMEM],
         out_specs=(VMEM,) * 4,
-        scratch_shapes=[pltpu.SemaphoreType.DMA((4,))],
         compiler_params=small,
     )(objects)
     lower0 = passed_along(lower0, "row", -1)
-    corner = passed_across(corner, -1)
+    corner = [passed_across(corner, -1)]
     right0 = passed_along(right0, "col", -1)
-    received = []
-    for by in range(1, mode_count):
-        received.append(lax.ppermute(probes, "mode", [(i, (i + by) % mode_count) for i in range(mode_count)])[0])
-
+    received = [passed_round(probes, by)[0] for by in range(1, mode_count)]
+    corner += [passed_round(corner[0], by) for by in range(1, mode_count)]
     lower1 = pl.pallas_call(
         stage_kernel, out_shape=rim_lower, in_specs=[VMEM], out_specs=VMEM, compiler_params=small
     )(tile)
@@ -322,22 +326,22 @@
     middle = pl.pallas_call(
         middle_kernel,
         out_shape=waves,
-        in_specs=[SMEM] + [VMEM] * 6,
+        in_specs=[SMEM] + [VMEM] * (5 + mode_count),
         out_specs=VMEM,
         scratch_shapes=[window_area],
         compiler_params=params,
         cost_estimate=cost(12 * count * mode_count, n),
-    )(starts, tile, right0, lower0, corner, factors, table)
+    )(starts, tile, right0, lower0, factors, table, *corner)
 
     back, own1, grad_right1, grad_lower1, grad_corner1 = pl.pallas_call(
         second_kernel,
         out_shape=(waves, shape(2, t, t), shape(2, t, n), rim_lower, shape(2, n, n)),
-        in_specs=[SMEM] + [VMEM] * 7,
+        in_specs=[SMEM] + [VMEM] * (6 + mode_count),
         out_specs=(VMEM,) * 5,
         scratch_shapes=[window_area] * 2,
         compiler_params=params,
         cost_estimate=cost(6 * count * mode_count, n),
-    )(starts, tile, right1, lower1, corner, middle, targets, table)
+    )(starts, tile, right1, lower1, middle, targets, table, *corner)
     grad_lower1 = passed_along(grad_lower1, "row", 1)
     own0, grad_right, grad_lower0, grad_corner = pl.pallas_call(
         first_kernel,
@@ -363,8 +367,8 @@
             cost_estimate=cost(weight, n),
         )(own, lower)
 
-    own1 = with_lower(own1, grad_lower1, 20)
-    own0 = with_lower(own0, grad_lower0, 90)
+    own1 = with_lower(own1, grad_lower1, 60)
+    own0 = with_lower(own0, grad_lower0, 0)
     own = pl.pallas_call(
         add_right_kernel,
         out_shape=shape(*objects.shape),

time: 55.5 us -> 55.9 us (level)
  starting transfers between devices: 25.2 us -> 28.6 us
  waiting for transfers between devices: 10.2 us -> 7.54 us
    ppermute x1 -> x2, waiting for transfers between devices: 2.79 us -> 0.46 us  [passed_round(): lax.ppermute(value, 'mode', [(i, (i + by) % count) for i in range(count)])]
    ppermute x1 -> x2, starting transfers between devices: 3 us -> 5.21 us  [passed_round(): lax.ppermute(value, 'mode', [(i, (i + by) % count) for i in range(count)])]
    ppermute x7, starting transfers between devices: 15.4 us -> 16.5 us  [passed_along(): return lax.ppermute(value, axis, pairs)]
    pallas_call x1, Pallas kernels: 0.87 us -> 0.11 us  [on_device(): pl.pallas_call(pack_kernel, out_shape=(shape(*objects.shape), rim_lower,...]
  transfers between devices with their start and end apart: 10 -> 11, of which waited for: 4 -> 5; matrix products, arithmetic and copies ran while one was open for 0% -> 0% of each run, Pallas kernels for 20% -> 11%
where the time goes in v4:
time: 55.9 us; the launch traced here: 55.6 us
  starting transfers between devices  28.6 us (51%)
  Pallas kernels  17.9 us (32%)
  waiting for transfers between devices  7.54 us (13%)
  local copies, waits for them, and re-layouts  1.32 us (2%)
    ppermute x7, starting transfers between devices, passed_along(): return lax.ppermute(value, axis, pairs)  16.5 us
    ppermute x2, starting transfers between devices, passed_across(): return lax.ppermute(value, ('row', 'col'), pairs)  6.81 us
    pallas_call x1, Pallas kernels, on_device(): pl.pallas_call(second_kernel, out_shape=(waves, shape(2, t, t), shape(2,...  5.82 us
    ppermute x2, waiting for transfers between devices, passed_across(): return lax.ppermute(value, ('row', 'col'), pairs)  5.72 us
    ppermute x2, starting transfers between devices, passed_round(): lax.ppermute(value, 'mode', [(i, (i + by) % count) for i in range(count)])  5.21 us
    pallas_call x1, Pallas kernels, on_device(): pl.pallas_call(middle_kernel, out_shape=waves, in_specs=[SMEM] + [VMEM] *...  5.19 us
    pallas_call x1, Pallas kernels, on_device(): pl.pallas_call(first_kernel, out_shape=(shape(2, t, t), rim_right, rim_lo...  5.02 us
    ppermute x7, waiting for transfers between devices, passed_along(): return lax.ppermute(value, axis, pairs)  1.36 us
  transfers between devices with their start and end apart: 11, of which 5 were waited for; matrix products, arithmetic and copies ran while one was open for 0% of the time, Pallas kernels for 11%

profile of v4, /device:TPU:0, one launch (start us, length us, event | category | flops | bytes accessed | tf_op | source)
XLA Modules:
  0.0 55.6 jit_solution(10231414094500795413)
XLA Ops:
  0.0 0.0 copy-start
  0.0 1.2 %copy-done = f32[2,2,256,256]{3,2,1,0:T(8,128)S(1)} copy-done((f32[2,2,256,256]{3,2,1,0:T(8,128)S(1)}, f32[2,2,256,256]{3,2,1,0:T(8,128)}, u32[]{:S(2)}) %copy-start) | copy-done | bytes 1048600
  1.2 0.0 copy-start.5
  1.2 0.0 copy-start.1
  1.2 0.0 copy-start.2
  1.2 0.0 copy-start.3
  1.2 0.1 shard_map.64
  1.4 1.4 %collective-permute-start.5 = (f32[2,2,64,128]{3,2,1,0:T(8,128)S(1)}, f32[2,2,64,128]{3,2,1,0:T(8,128)}, u32[]{:S(2)}, u32[]{:S(2)}) collective-permute-start(f32[2,2,64,128]{3,2,1,0:T(8,128)S(1)} %get-tuple-element.27), channel_id=1, source_target_pairs={{10,0},{12,2},{14,4},{18,8},{20,10},{22,12},{26,16},{28,18},{30,20... | collective-permute-start | bytes 393224 | tf_op jit(solution)/shard_map/ppermute | solution.py:39
  2.8 1.3 %collective-permute-start.3 = (f32[2,256,128]{2,1,0:T(8,128)S(1)}, f32[2,256,128]{2,1,0:T(8,128)S(1)}, u32[]{:S(2)}, u32[]{:S(2)}) collective-permute-start(f32[2,256,128]{2,1,0:T(8,128)S(1)} %get-tuple-element.23), channel_id=1, source_target_pairs={{2,0},{4,2},{6,4},{3,1},{5,3},{7,5},{10,8},{12,10},{14,12},{11,9},... | collective-permute-start | bytes 786440 | tf_op jit(solution)/shard_map/ppermute | solution.py:23
  4.1 1.3 %collective-permute-start.4 = (f32[2,128,256]{2,1,0:T(8,128)S(1)}, f32[2,128,256]{2,1,0:T(8,128)S(1)}, u32[]{:S(2)}, u32[]{:S(2)}) collective-permute-start(f32[2,128,256]{2,1,0:T(8,128)S(1)} %get-tuple-element.24), channel_id=1, source_target_pairs={{8,0},{16,8},{24,16},{9,1},{17,9},{25,17},{10,2},{18,10},{26,18},{... | collective-permute-start | bytes 786440 | tf_op jit(solution)/shard_map/ppermute | solution.py:23
  5.4 3.0 %collective-permute-start = (f32[1,2,128,128]{3,2,1,0:T(8,128)}, f32[1,2,128,128]{3,2,1,0:T(8,128)S(1)}, u32[]{:S(2)}, u32[]{:S(2)}) collective-permute-start(f32[1,2,128,128]{3,2,1,0:T(8,128)} %param.7), channel_id=1, source_target_pairs={{0,1},{1,0},{2,3},{3,2},{4,5},{5,4},{6,7},{7,6},{8,9},{9,8},{10,11... | collective-permute-start | bytes 393224 | tf_op jit(solution)/shard_map/ppermute | solution.py:28
  8.4 0.2 collective-permute-done.5.refs_0_
  8.6 2.2 %collective-permute-start.6 = (f32[2,2,64,128]{3,2,1,0:T(8,128)}, f32[2,2,64,128]{3,2,1,0:T(8,128)}, u32[]{:S(2)}, u32[]{:S(2)}) collective-permute-start(f32[2,2,64,128]{3,2,1,0:T(8,128)} %collective-permute-done.5.refs_0_), channel_id=1, source_target_pairs={{0,1},{1,0},{2,3},{3,2},{4,5},{5,4},{6,7},{7,6},{8,9},{9,8},{10,11... | collective-permute-start | bytes 393224 | tf_op jit(solution)/shard_map/ppermute | solution.py:28
  10.8 1.3 %collective-permute-start.2 = (f32[2,128,256]{2,1,0:T(8,128)S(1)}, f32[2,128,256]{2,1,0:T(8,128)S(1)}, u32[]{:S(2)}, u32[]{:S(2)}) collective-permute-start(f32[2,128,256]{2,1,0:T(8,128)S(1)} %shard_map.66), channel_id=1, source_target_pairs={{8,0},{16,8},{24,16},{9,1},{17,9},{25,17},{10,2},{18,10},{26,18},{... | collective-permute-start | bytes 786440 | tf_op jit(solution)/shard_map/ppermute | solution.py:23
  12.1 0.0 copy-done.5
  12.2 0.1 copy.11.offsets
  12.2 0.4 collective-permute-done
  12.6 0.0 copy-done.1
  12.6 0.0 copy-done.2
  12.6 0.0 copy-done.3
  12.6 0.5 shard_map.65
  13.1 1.3 %collective-permute-start.1 = (f32[2,256,128]{2,1,0:T(8,128)S(1)}, f32[2,256,128]{2,1,0:T(8,128)S(1)}, u32[]{:S(2)}, u32[]{:S(2)}) collective-permute-start(f32[2,256,128]{2,1,0:T(8,128)S(1)} %get-tuple-element.22), channel_id=1, source_target_pairs={{2,0},{4,2},{6,4},{3,1},{5,3},{7,5},{10,8},{12,10},{14,12},{11,9},... | collective-permute-start | bytes 786440 | tf_op jit(solution)/shard_map/ppermute | solution.py:23
  14.4 0.1 collective-permute-done.6.refs_1_
  14.5 0.0 collective-permute-done.3.right
  14.5 1.3 %collective-permute-done.4.lower = f32[2,128,256]{2,1,0:T(8,128)S(1)} collective-permute-done((f32[2,128,256]{2,1,0:T(8,128)S(1)}, f32[2,128,256]{2,1,0:T(8,128)S(1)}, u32[]{:S(2)}, u32[]{:S(2)}) %collective-permute-start.4) | collective-permute-done | bytes 262176 | tf_op jit(solution)/shard_map/ppermute | solution.py:23
  15.8 0.0 copy-start.4
  15.8 5.2 %shard_map.67.middle = f32[8,2,2,128,128]{4,3,2,1,0:T(8,128)S(1)} custom-call(s32[8,2]{1,0:T(8,128)S(1)} %copy.11.offsets, f32[2,2,256,256]{3,2,1,0:T(8,128)S(1)} %get-tuple-element.21.refs_2_.tile.objects, f32[2,256,128]{2,1,0:T(8,128)S(1)} %collective-permute-done.3.right, f32[2,128,256]{2,1,0:T(8,128)S(1)} %collective-permute-done.4.lower, ...), custom_call_target="tpu_custom_call" | custom-call | flops 9663676416 | bytes 4194304 | tf_op jit(solution)/shard_map/pallas_call | solution.py:326
  21.0 0.0 collective-permute-done.2.lower
  21.0 0.0 collective-permute-done.1.right
  21.0 0.0 copy-done.4
  21.1 5.8 %shard_map.68 = (f32[8,2,2,128,128]{4,3,2,1,0:T(8,128)S(1)}, f32[2,256,256]{2,1,0:T(8,128)S(1)}, f32[2,256,128]{2,1,0:T(8,128)S(1)}, f32[2,128,256]{2,1,0:T(8,128)S(1)}, f32[2,128,128]{2,1,0:T(8,128)S(1)}) custom-call(s32[8,2]{1,0:T(8,128)S(1)} %copy.11.offsets, f32[2,2,256,256]{3,2,1,0:T(8,128)S(1)} %get-tuple-element.21.refs_2_.tile.objects, ...), custom_call_target="tpu_custom_call" | custom-call | flops 4831838208 | bytes 4194304 | tf_op jit(solution)/shard_map/pallas_call | solution.py:336
  26.9 5.0 %shard_map.69 = (f32[2,256,256]{2,1,0:T(8,128)S(1)}, f32[2,2,256,128]{3,2,1,0:T(8,128)S(1)}, f32[2,128,256]{2,1,0:T(8,128)S(1)}, f32[2,2,128,128]{3,2,1,0:T(8,128)S(1)}) custom-call(s32[8,2]{1,0:T(8,128)S(1)} %copy.11.offsets, f32[8,2,2,128,128]{4,3,2,1,0:T(8,128)S(1)} %get-tuple-element.28.back, f32[3,2,128,128]{3,2,1,0:T(8,128)S(1)} %get-tuple-element.25.factors, ...), custom_call_target="tpu_custom_call" | custom-call | flops 4831838208 | bytes 4194304 | tf_op jit(solution)/shard_map/pallas_call | solution.py:346
  31.9 4.2 %collective-permute-start.7 = (f32[2,128,256]{2,1,0:T(8,128)S(1)}, f32[2,128,256]{2,1,0:T(8,128)S(1)}, u32[]{:S(2)}, u32[]{:S(2)}) collective-permute-start(f32[2,128,256]{2,1,0:T(8,128)S(1)} %get-tuple-element.32), channel_id=1, source_target_pairs={{0,8},{8,16},{16,24},{1,9},{9,17},{17,25},{2,10},{10,18},{18,26},{... | collective-permute-start | bytes 786440 | tf_op jit(solution)/shard_map/ppermute | solution.py:23
  36.1 4.1 %collective-permute-start.8 = (f32[2,128,256]{2,1,0:T(8,128)S(1)}, f32[2,128,256]{2,1,0:T(8,128)S(1)}, u32[]{:S(2)}, u32[]{:S(2)}) collective-permute-start(f32[2,128,256]{2,1,0:T(8,128)S(1)} %get-tuple-element.34), channel_id=1, source_target_pairs={{0,8},{8,16},{16,24},{1,9},{9,17},{17,25},{2,10},{10,18},{18,26},{... | collective-permute-start | bytes 786440 | tf_op jit(solution)/shard_map/ppermute | solution.py:23
  40.2 3.1 %collective-permute-start.9 = (f32[2,2,256,128]{3,2,1,0:T(8,128)S(1)}, f32[2,2,256,128]{3,2,1,0:T(8,128)S(1)}, u32[]{:S(2)}, u32[]{:S(2)}) collective-permute-start(f32[2,2,256,128]{3,2,1,0:T(8,128)S(1)} %get-tuple-element.35), channel_id=1, source_target_pairs={{0,2},{2,4},{4,6},{1,3},{3,5},{5,7},{8,10},{10,12},{12,14},{9,11},... | collective-permute-start | bytes 1572872 | tf_op jit(solution)/shard_map/ppermute | solution.py:23
  43.3 5.4 %collective-permute-start.10 = (f32[2,2,128,128]{3,2,1,0:T(8,128)S(1)}, f32[2,2,128,128]{3,2,1,0:T(8,128)S(1)}, u32[]{:S(2)}, u32[]{:S(2)}) collective-permute-start(f32[2,2,128,128]{3,2,1,0:T(8,128)S(1)} %get-tuple-element.36), channel_id=1, source_target_pairs={{0,10},{2,12},{4,14},{8,18},{10,20},{12,22},{16,26},{18,28},{20,30... | collective-permute-start | bytes 786440 | tf_op jit(solution)/shard_map/ppermute | solution.py:39
  48.7 0.0 collective-permute-done.7.lower
  48.7 0.1 shard_map.70.own0
  48.8 0.0 collective-permute-done.8.lower
  48.8 0.1 shard_map.71.own1
  48.9 0.0 collective-permute-done.9.right
  48.9 0.1 shard_map.72.own
  49.0 5.5 %collective-permute-done.10.corner = f32[2,2,128,128]{3,2,1,0:T(8,128)S(1)} collective-permute-done((f32[2,2,128,128]{3,2,1,0:T(8,128)S(1)}, f32[2,2,128,128]{3,2,1,0:T(8,128)S(1)}, u32[]{:S(2)}, u32[]{:S(2)}) %collective-permute-start.10) | collective-permute-done | bytes 262176 | tf_op jit(solution)/shard_map/ppermute | solution.py:39
  54.5 1.0 %shard_map.73 = f32[2,2,256,256]{3,2,1,0:T(8,128)} custom-call(f32[2,2,256,256]{3,2,1,0:T(8,128)S(1)} %shard_map.72.own, f32[2,2,128,128]{3,2,1,0:T(8,128)S(1)} %collective-permute-done.10.corner), custom_call_target="tpu_custom_call" | custom-call | tf_op jit(solution)/shard_map/pallas_call | solution.py:380
  (1 shorter events, 0.0 us)
Async XLA Ops:
  0.0 1.2 %copy-start = (f32[2,2,256,256]{3,2,1,0:T(8,128)S(1)}, f32[2,2,256,256]{3,2,1,0:T(8,128)}, u32[]{:S(2)}) copy-start(f32[2,2,256,256]{3,2,1,0:T(8,128)} %objects.1) | copy-start | bytes 3145732
  1.2 10.9 %copy-start.5 = (s32[1,1,8,2]{2,3,1,0:T(2,128)S(1)}, s32[1,1,8,2]{2,3,1,0:T(2,128)}, u32[]{:S(2)}) copy-start(s32[1,1,8,2]{2,3,1,0:T(2,128)} %param.9) | copy-start | bytes 196
  1.2 11.4 %copy-start.1 = (bf16[2,2,256,256]{3,2,1,0:T(8,128)(2,1)S(1)}, bf16[2,2,256,256]{3,2,1,0:T(8,128)(2,1)}, u32[]{:S(2)}) copy-start(bf16[2,2,256,256]{3,2,1,0:T(8,128)(2,1)} %constant.2.clone.refs_4_) | copy-start | bytes 1572868
  1.2 11.4 %copy-start.2 = (f32[1,2,128,128]{3,2,1,0:T(8,128)S(1)}, f32[1,2,128,128]{3,2,1,0:T(8,128)}, u32[]{:S(2)}) copy-start(f32[1,2,128,128]{3,2,1,0:T(8,128)} %param.7) | copy-start | bytes 393220
  1.2 11.4 %copy-start.3 = (f32[128,128]{1,0:T(8,128)S(1)}, f32[128,128]{1,0:T(8,128)}, u32[]{:S(2)}) copy-start(f32[128,128]{1,0:T(8,128)} %refs_3_.1) | copy-start | bytes 196612
  1.4 7.3 %collective-permute-start.5 = (f32[2,2,64,128]{3,2,1,0:T(8,128)S(1)}, f32[2,2,64,128]{3,2,1,0:T(8,128)}, u32[]{:S(2)}, u32[]{:S(2)}) collective-permute-start(f32[2,2,64,128]{3,2,1,0:T(8,128)S(1)} %get-tuple-element.27), channel_id=1, source_target_pairs={{10,0},{12,2},{14,4},{18,8},{20,10},{22,12},{26,16},{28,18},{30,20... | collective-permute-start | bytes 393224 | tf_op jit(solution)/shard_map/ppermute | solution.py:39
  2.8 11.7 %collective-permute-start.3 = (f32[2,256,128]{2,1,0:T(8,128)S(1)}, f32[2,256,128]{2,1,0:T(8,128)S(1)}, u32[]{:S(2)}, u32[]{:S(2)}) collective-permute-start(f32[2,256,128]{2,1,0:T(8,128)S(1)} %get-tuple-element.23), channel_id=1, source_target_pairs={{2,0},{4,2},{6,4},{3,1},{5,3},{7,5},{10,8},{12,10},{14,12},{11,9},... | collective-permute-start | bytes 786440 | tf_op jit(solution)/shard_map/ppermute | solution.py:23
  4.1 11.7 %collective-permute-start.4 = (f32[2,128,256]{2,1,0:T(8,128)S(1)}, f32[2,128,256]{2,1,0:T(8,128)S(1)}, u32[]{:S(2)}, u32[]{:S(2)}) collective-permute-start(f32[2,128,256]{2,1,0:T(8,128)S(1)} %get-tuple-element.24), channel_id=1, source_target_pairs={{8,0},{16,8},{24,16},{9,1},{17,9},{25,17},{10,2},{18,10},{26,18},{... | collective-permute-start | bytes 786440 | tf_op jit(solution)/shard_map/ppermute | solution.py:23
  5.4 7.2 %collective-permute-start = (f32[1,2,128,128]{3,2,1,0:T(8,128)}, f32[1,2,128,128]{3,2,1,0:T(8,128)S(1)}, u32[]{:S(2)}, u32[]{:S(2)}) collective-permute-start(f32[1,2,128,128]{3,2,1,0:T(8,128)} %param.7), channel_id=1, source_target_pairs={{0,1},{1,0},{2,3},{3,2},{4,5},{5,4},{6,7},{7,6},{8,9},{9,8},{10,11... | collective-permute-start | bytes 393224 | tf_op jit(solution)/shard_map/ppermute | solution.py:28
  8.6 5.9 %collective-permute-start.6 = (f32[2,2,64,128]{3,2,1,0:T(8,128)}, f32[2,2,64,128]{3,2,1,0:T(8,128)}, u32[]{:S(2)}, u32[]{:S(2)}) collective-permute-start(f32[2,2,64,128]{3,2,1,0:T(8,128)} %collective-permute-done.5.refs_0_), channel_id=1, source_target_pairs={{0,1},{1,0},{2,3},{3,2},{4,5},{5,4},{6,7},{7,6},{8,9},{9,8},{10,11... | collective-permute-start | bytes 393224 | tf_op jit(solution)/shard_map/ppermute | solution.py:28
  10.8 10.2 %collective-permute-start.2 = (f32[2,128,256]{2,1,0:T(8,128)S(1)}, f32[2,128,256]{2,1,0:T(8,128)S(1)}, u32[]{:S(2)}, u32[]{:S(2)}) collective-permute-start(f32[2,128,256]{2,1,0:T(8,128)S(1)} %shard_map.66), channel_id=1, source_target_pairs={{8,0},{16,8},{24,16},{9,1},{17,9},{25,17},{10,2},{18,10},{26,18},{... | collective-permute-start | bytes 786440 | tf_op jit(solution)/shard_map/ppermute | solution.py:23
  13.1 8.0 %collective-permute-start.1 = (f32[2,256,128]{2,1,0:T(8,128)S(1)}, f32[2,256,128]{2,1,0:T(8,128)S(1)}, u32[]{:S(2)}, u32[]{:S(2)}) collective-permute-start(f32[2,256,128]{2,1,0:T(8,128)S(1)} %get-tuple-element.22), channel_id=1, source_target_pairs={{2,0},{4,2},{6,4},{3,1},{5,3},{7,5},{10,8},{12,10},{14,12},{11,9},... | collective-permute-start | bytes 786440 | tf_op jit(solution)/shard_map/ppermute | solution.py:23
  15.8 5.2 %copy-start.4 = (f32[1,1,8,128,128]{4,3,2,1,0:T(8,128)S(1)}, f32[1,1,8,128,128]{4,3,2,1,0:T(8,128)}, u32[]{:S(2)}) copy-start(f32[1,1,8,128,128]{4,3,2,1,0:T(8,128)} %param.10) | copy-start | bytes 1572868
  31.9 16.8 %collective-permute-start.7 = (f32[2,128,256]{2,1,0:T(8,128)S(1)}, f32[2,128,256]{2,1,0:T(8,128)S(1)}, u32[]{:S(2)}, u32[]{:S(2)}) collective-permute-start(f32[2,128,256]{2,1,0:T(8,128)S(1)} %get-tuple-element.32), channel_id=1, source_target_pairs={{0,8},{8,16},{16,24},{1,9},{9,17},{17,25},{2,10},{10,18},{18,26},{... | collective-permute-start | bytes 786440 | tf_op jit(solution)/shard_map/ppermute | solution.py:23
  36.1 12.7 %collective-permute-start.8 = (f32[2,128,256]{2,1,0:T(8,128)S(1)}, f32[2,128,256]{2,1,0:T(8,128)S(1)}, u32[]{:S(2)}, u32[]{:S(2)}) collective-permute-start(f32[2,128,256]{2,1,0:T(8,128)S(1)} %get-tuple-element.34), channel_id=1, source_target_pairs={{0,8},{8,16},{16,24},{1,9},{9,17},{17,25},{2,10},{10,18},{18,26},{... | collective-permute-start | bytes 786440 | tf_op jit(solution)/shard_map/ppermute | solution.py:23
  40.2 8.7 %collective-permute-start.9 = (f32[2,2,256,128]{3,2,1,0:T(8,128)S(1)}, f32[2,2,256,128]{3,2,1,0:T(8,128)S(1)}, u32[]{:S(2)}, u32[]{:S(2)}) collective-permute-start(f32[2,2,256,128]{3,2,1,0:T(8,128)S(1)} %get-tuple-element.35), channel_id=1, source_target_pairs={{0,2},{2,4},{4,6},{1,3},{3,5},{5,7},{8,10},{10,12},{12,14},{9,11},... | collective-permute-start | bytes 1572872 | tf_op jit(solution)/shard_map/ppermute | solution.py:23
  43.3 11.2 %collective-permute-start.10 = (f32[2,2,128,128]{3,2,1,0:T(8,128)S(1)}, f32[2,2,128,128]{3,2,1,0:T(8,128)S(1)}, u32[]{:S(2)}, u32[]{:S(2)}) collective-permute-start(f32[2,2,128,128]{3,2,1,0:T(8,128)S(1)} %get-tuple-element.36), channel_id=1, source_target_pairs={{0,10},{2,12},{4,14},{8,18},{10,20},{12,22},{16,26},{18,28},{20,30... | collective-permute-start | bytes 786440 | tf_op jit(solution)/shard_map/ppermute | solution.py:39
